TPU v7x, 256 devices: a whole 4x4x8 slice. The times are simulated.
256 devices in a mesh: dp: 16 (over y, x_hi, core), space: 16 (over z, x_lo).
Axes of the slice: x: 4 (x_hi: 2, x_lo: 2; x = x_hi * 2 + x_lo), y: 4, z: 8, core: 2. Of those that a mesh axis runs over, the one named last changes fastest.
Arguments:
- features: bfloat16 [16, 64, 64, 512], P('dp', 'space'), may hold values from -45 to 45
- timestep: int32 [16], P('dp'), may hold values from 0 to 999
- w_time: bfloat16 [128, 512], replicated, may hold values from -0.5 to 0.5
- w_emb: bfloat16 [512, 1024], replicated, may hold values from -0.25 to 0.25
- w_qkv: bfloat16 [512, 1536], replicated, may hold values from -1.125 to 1.125
- w_out: bfloat16 [512, 512], replicated, may hold values from -0.25 to 0.25
- w_conv: bfloat16 [4608, 512], replicated, may hold values from -0.09375 to 0.09375
- upstream: bfloat16 [16, 64, 64, 512], P('dp', 'space'), may hold values from -6 to 6
Outputs:
- output: bfloat16 [16, 64, 64, 512], P('dp', 'space')
- grad_features: bfloat16 [16, 64, 64, 512], P('dp', 'space')
- grad_conv: float32 [2359296], P(('dp', 'space'))
- grad_out: float32 [262144], P(('dp', 'space'))
All inputs are finite; a program needn't handle non-finite values.
Results may differ from a plain program's by a relative error of at most 0.015.
The roundings to bfloat16 on the way count: a program that leaves them out, or rounds other values in their place, can miss the bound.
Values may be sent and summed in bfloat16 or wider, within the bound.
A program may use at most 128 MiB of HBM per device.

v0:
```python
import math

import jax
import jax.numpy as jnp
from jax import lax
from jax.sharding import PartitionSpec as P

HEADS = 8
HEAD_DIM = 64
GROUPS = 32
TFEAT = 128
SIDE = 64


epsilon = 1e-05


def with_halo(block, sides, width):
    for axis, dim in sides:
        count = lax.axis_size(axis)
        forward = [(i, i + 1) for i in range(count - 1)]
        backward = [(target, source) for source, target in forward]
        low = lax.ppermute(
            lax.slice_in_dim(block, block.shape[dim] - width, None, axis=dim), axis, forward
        )
        high = lax.ppermute(lax.slice_in_dim(block, 0, width, axis=dim), axis, backward)
        block = jnp.concatenate([low, block, high], axis=dim)
    return block


def single_sum(partial_value):
    return lax.psum(partial_value, "space")


def pair_sums(first, second):
    return lax.psum((first, second), "space")


def group_norm(values):
    images, rows, cols, width = values.shape
    grouped = values.reshape(images, rows * cols, GROUPS, width // GROUPS)
    count = SIDE * SIDE * (width // GROUPS)
    center = single_sum(jnp.sum(grouped, axis=(1, 3))) / count
    offsets = grouped - center[:, None, :, None]
    spread = single_sum(jnp.sum(offsets * offsets, axis=(1, 3))) / count
    inverse = lax.rsqrt(spread + epsilon)
    return (offsets * inverse[:, None, :, None], inverse)


def time_features(timestep):
    halfway = TFEAT // 2
    frequency = jnp.exp(-math.log(10000.0) * jnp.arange(halfway, dtype=jnp.float32) / halfway)
    angles = timestep.astype(jnp.float32)[:, None] * frequency[None, :]
    return jnp.concatenate([jnp.cos(angles), jnp.sin(angles)], axis=1)


def with_margins(values):
    padded = with_halo(values, (("space", 1),), 1)
    return jnp.pad(padded, ((0, 0), (0, 0), (1, 1), (0, 0)))


def reduce_grads(conv_part, out_part):
    return (
        lax.psum_scatter(conv_part, ("dp", "space"), scatter_dimension=0, tiled=True),
        lax.psum_scatter(out_part, ("dp", "space"), scatter_dimension=0, tiled=True),
    )


def attend_blocks(carry, queries, keys, values):
    image_count = keys.shape[0]
    key_count = keys.shape[1]
    head_count = keys.shape[2]
    head_width = keys.shape[3]
    block = 512
    blocks = key_count // block
    key_blocks = keys.reshape(image_count, blocks, block, head_count, head_width).transpose(
        1, 0, 2, 3, 4
    )
    value_blocks = values.reshape(image_count, blocks, block, head_count, head_width).transpose(
        1, 0, 2, 3, 4
    )

    def advance(state, pair):
        running_top, running_total, accum = state
        key_block, value_block = pair
        scores = jnp.einsum(
            "iqhd,ikhd->ihqk", queries, key_block, preferred_element_type=jnp.float32
        ) / math.sqrt(HEAD_DIM)
        new_top = jnp.maximum(running_top, jnp.max(scores, axis=3))
        weights = jnp.exp(scores - new_top[..., None])
        shrink = jnp.exp(running_top - new_top)
        running_total = running_total * shrink + jnp.sum(weights, axis=3)
        accum = accum * shrink[..., None] + jnp.einsum(
            "ihqk,ikhd->ihqd",
            weights.astype(jnp.bfloat16),
            value_block,
            preferred_element_type=jnp.float32,
        )
        return ((new_top, running_total, accum), None)

    state, unused_out = lax.scan(advance, carry, (key_blocks, value_blocks))
    return state


def on_device(features, timestep, w_time, w_emb, w_qkv, w_out, w_conv, upstream):
    images, rows, cols, width = features.shape
    tokens = rows * cols
    embedded = jnp.dot(
        time_features(timestep), w_time.astype(jnp.float32), precision=lax.Precision.HIGHEST
    )
    shifts_all = jnp.dot(
        jax.nn.silu(embedded), w_emb.astype(jnp.float32), precision=lax.Precision.HIGHEST
    )
    scale_rows = shifts_all[:, None, None, :width]
    shift_rows = shifts_all[:, None, None, width:]
    normed_groups, unused = group_norm(features.astype(jnp.float32))
    normed = normed_groups.reshape(images, tokens, width).astype(jnp.bfloat16)
    projected = jnp.einsum("itc,cd->itd", normed, w_qkv, preferred_element_type=jnp.float32).astype(
        jnp.bfloat16
    )
    queries_flat = projected[..., :width]
    queries = queries_flat.reshape(images, tokens, HEADS, HEAD_DIM)
    initial = (
        jnp.full((images, HEADS, tokens), -jnp.inf, jnp.float32),
        jnp.zeros((images, HEADS, tokens), jnp.float32),
        jnp.zeros((images, HEADS, tokens, HEAD_DIM), jnp.float32),
    )
    pieces = (
        lax.all_gather(projected[..., width : 2 * width], "space", axis=1, tiled=True),
        lax.all_gather(projected[..., 2 * width :], "space", axis=1, tiled=True),
    )
    key_part = pieces[0].reshape(images, pieces[0].shape[1], HEADS, HEAD_DIM)
    value_part = pieces[1].reshape(images, pieces[1].shape[1], HEADS, HEAD_DIM)
    final_top, final_total, final_accum = attend_blocks(initial, queries, key_part, value_part)
    attended = (
        (final_accum / final_total[..., None])
        .transpose(0, 2, 1, 3)
        .reshape(images, tokens, width)
        .astype(jnp.bfloat16)
    )
    hidden = (
        features.astype(jnp.float32)
        + jnp.einsum("itc,cd->itd", attended, w_out, preferred_element_type=jnp.float32).reshape(
            features.shape
        )
    ).astype(jnp.bfloat16)
    hat_groups, inverse = group_norm(hidden.astype(jnp.float32))
    hat = hat_groups.reshape(features.shape)
    shifted = hat * (1.0 + scale_rows) + shift_rows
    activated = jax.nn.silu(shifted).astype(jnp.bfloat16)
    padded = with_margins(activated)
    padded_grad = with_margins(upstream)
    result = jnp.zeros((images, rows, cols, width), jnp.float32)
    back = jnp.zeros((images, rows, cols, width), jnp.float32)
    pieces_list = []
    for position in range(9):
        row_step = position // 3
        col_step = position % 3
        window = padded[:, row_step : row_step + rows, col_step : col_step + cols]
        kernel = w_conv[position * width : (position + 1) * width]
        result = result + jnp.einsum(
            "irsc,cd->irsd", window, kernel, preferred_element_type=jnp.float32
        )
        pieces_list.append(
            jnp.einsum("irsc,irsd->cd", window, upstream, preferred_element_type=jnp.float32)
        )
        moved = padded_grad[
            :, 2 - row_step : 2 - row_step + rows, 2 - col_step : 2 - col_step + cols
        ]
        back = back + jnp.einsum("irsd,cd->irsc", moved, kernel, preferred_element_type=jnp.float32)
    output = result.astype(jnp.bfloat16)
    sigma = jax.nn.sigmoid(shifted)
    through = back * sigma * (1.0 + shifted * (1.0 - sigma)) * (1.0 + scale_rows)
    through_groups = through.reshape(hat_groups.shape)
    count = SIDE * SIDE * (width // GROUPS)
    first, second = pair_sums(
        jnp.sum(through_groups, axis=(1, 3)), jnp.sum(through_groups * hat_groups, axis=(1, 3))
    )
    first_mean = first / count
    second_mean = second / count
    grad_hidden = inverse[:, None, :, None] * (
        through_groups - first_mean[:, None, :, None] - hat_groups * second_mean[:, None, :, None]
    )
    grad_features = grad_hidden.reshape(features.shape).astype(jnp.bfloat16)
    out_part = jnp.einsum(
        "itc,itd->cd",
        attended,
        grad_features.reshape(images, tokens, width),
        preferred_element_type=jnp.float32,
    ).reshape(-1)
    conv_part = jnp.concatenate(pieces_list, axis=0).reshape(-1)
    grad_conv, grad_out = reduce_grads(conv_part, out_part)
    return (output, grad_features, grad_conv, grad_out)


def solution(mesh):
    return jax.shard_map(
        on_device,
        mesh=mesh,
        in_specs=(
            P("dp", "space", None, None),
            P("dp"),
            P(),
            P(),
            P(),
            P(),
            P(),
            P("dp", "space", None, None),
        ),
        out_specs=(
            P("dp", "space", None, None),
            P("dp", "space", None, None),
            P(("dp", "space")),
            P(("dp", "space")),
        ),
        check_vma=False,
    )
```

profile of v0, /device:TPU:1, one launch (start us, length us, event | category | flops | bytes accessed | tf_op | source)
XLA Modules:
  0.0 794.6 jit_solution(12005558225086806223)
XLA Ops:
  8.6 31.2 %psum.42 = f32[1,32]{1,0:T(1,128)S(1)} all-reduce(f32[1,32]{1,0:T(1,128)S(1)} %bitcast.338), channel_id=1, replica_groups=mesh['dp'=16,'space'=16] {'space'}, use_global_device_ids=true, to_apply=%region_2.3 | all-reduce | flops 32 | bytes 256 | tf_op jit(solution)/shard_map/psum | solution.py:32
  41.2 23.7 %psum.43 = f32[1,32]{1,0:T(1,128)S(1)} all-reduce(f32[1,32]{1,0:T(1,128)S(1)} %bitcast.339), channel_id=1, replica_groups=mesh['dp'=16,'space'=16] {'space'}, use_global_device_ids=true, to_apply=%region_5.6 | all-reduce | flops 32 | bytes 256 | tf_op jit(solution)/shard_map/psum | solution.py:32
  69.7 4.3 collective-permute-start.2
  74.9 1.8 fusion.135
  77.0 2.3 fusion.50
  83.8 93.6 %all-gather.3.cloned.1.call-done = bf16[1,4096,512]{2,1,0:T(8,128)(2,1)} async-done(((bf16[1,256,512]{2,1,0:T(8,128)(2,1)}), bf16[1,4096,512]{2,1,0:T(8,128)(2,1)}) %all-gather.3.cloned.1.call-update) | async-done | bytes 4194320 | tf_op jit(solution)/shard_map/all_gather | solution.py:129
  177.4 11.2 %reshape.416 = bf16[8,1,512,8,64]{4,3,2,0,1:T(8,128)(2,1)} reshape(bf16[1,4096,512]{2,1,0:T(8,128)(2,1)} %all-gather.3.cloned.1.call-done) | data formatting | bytes 8388608 | tf_op jit(solution)/shard_map/transpose;reshape;reshape | solution.py:76
  188.6 9.7 %copy.28 = bf16[8,1,512,8,64]{2,4,3,1,0:T(8,128)(2,1)} copy(bf16[8,1,512,8,64]{4,3,2,0,1:T(8,128)(2,1)} %reshape.416) | data formatting | bytes 8388608
  198.3 80.3 %all-gather.5.cloned.1.call-done = bf16[1,4096,512]{2,1,0:T(8,128)(2,1)} async-done(((bf16[1,256,512]{2,1,0:T(8,128)(2,1)}), bf16[1,4096,512]{2,1,0:T(8,128)(2,1)}) %all-gather.5.cloned.1.call-update) | async-done | bytes 4194320 | tf_op jit(solution)/shard_map/all_gather | solution.py:130
  278.6 11.2 %reshape.417 = bf16[8,1,512,8,64]{4,3,2,0,1:T(8,128)(2,1)} reshape(bf16[1,4096,512]{2,1,0:T(8,128)(2,1)} %all-gather.5.cloned.1.call-done) | data formatting | bytes 8388608 | tf_op jit(solution)/shard_map/transpose;reshape;reshape | solution.py:79
  289.8 9.7 %copy.29 = bf16[8,1,512,8,64]{2,4,3,1,0:T(8,128)(2,1)} copy(bf16[8,1,512,8,64]{4,3,2,0,1:T(8,128)(2,1)} %reshape.417) | data formatting | bytes 8388608
  299.5 73.5 %while.15 = (s32[]{:T(128)}, f32[1,8,256]{2,1,0:T(8,128)S(1)}, f32[1,8,256]{2,1,0:T(8,128)S(1)}, f32[1,8,256,64]{2,3,1,0:T(8,128)S(1)}, bf16[8,1,512,8,64]{2,4,3...) while((s32[]{:T(128)}, f32[1,8,256]{2,1,0:T(8,128)S(1)}, ...), condition=%wide.region_9.10_spmd.clone, body=%wide.region_6.9_spmd.clone.sunk | while | flops 277229568 | bytes 31850644 | solution.py:101
  299.5 3.8 bitcast_reduce_fusion.2
  303.3 3.0 fusion.152
  306.7 2.0 fusion.153
  308.7 3.7 bitcast_reduce_fusion.2
  312.5 3.0 fusion.152
  315.9 2.0 fusion.153
  317.9 3.7 bitcast_reduce_fusion.2
  321.6 3.0 fusion.152
  325.1 2.0 fusion.153
  327.1 3.7 bitcast_reduce_fusion.2
  330.8 3.0 fusion.152
  334.3 2.0 fusion.153
  336.3 3.7 bitcast_reduce_fusion.2
  340.0 3.0 fusion.152
  343.5 2.0 fusion.153
  345.5 3.7 bitcast_reduce_fusion.2
  349.2 3.0 fusion.152
  352.6 2.0 fusion.153
  354.6 3.7 bitcast_reduce_fusion.2
  358.4 3.0 fusion.152
  361.8 2.0 fusion.153
  363.8 3.7 bitcast_reduce_fusion.2
  367.6 3.0 fusion.152
  371.0 2.0 fusion.153
  373.4 1.4 fusion.134
  375.0 26.9 %psum.44 = f32[1,32]{1,0:T(1,128)S(1)} all-reduce(f32[1,32]{1,0:T(1,128)S(1)} %bitcast.340), channel_id=1, replica_groups=mesh['dp'=16,'space'=16] {'space'}, use_global_device_ids=true, to_apply=%region_12.13 | all-reduce | flops 32 | bytes 256 | tf_op jit(solution)/shard_map/psum | solution.py:32
  402.3 24.0 %psum.45 = f32[1,32]{1,0:T(1,128)S(1)} all-reduce(f32[1,32]{1,0:T(1,128)S(1)} %bitcast.341), channel_id=1, replica_groups=mesh['dp'=16,'space'=16] {'space'}, use_global_device_ids=true, to_apply=%region_15.16 | all-reduce | flops 32 | bytes 256 | tf_op jit(solution)/shard_map/psum | solution.py:32
  426.5 1.7 fusion.44
  428.7 24.8 %all-reduce.5 = (f32[1,32]{1,0:T(1,128)S(1)}, f32[1,32]{1,0:T(1,128)S(1)}) all-reduce(f32[1,32]{1,0:T(1,128)S(1)} %bitcast.336, f32[1,32]{1,0:T(1,128)S(1)} %bitcast.337), channel_id=1, replica_groups=mesh['dp'=16,'space'=16] {'space'}, use_global_device_ids=true, to_apply=%region_21.22 | all-reduce | flops 64 | bytes 512 | tf_op jit(solution)/shard_map/psum | solution.py:36
  455.4 4.2 collective-permute-start
  464.2 3.6 copy-done.5
  467.9 9.7 %copy.37 = f32[576,4,8,128]{3,1,2,0:T(4,128)} copy(f32[576,4,8,128]{3,2,1,0:T(8,128)} %bitcast.322) | data formatting | bytes 18874368
  481.7 1.5 convolution_add_fusion.12
  488.6 2.1 fusion.42
  490.7 294.7 %all-reduce.8.cloned.1.call-done = (f32[2359296]{0:T(1024)}, f32[262144]{0:T(1024)}) async-done(((f32[2359296]{0:T(1024)}, f32[262144]{0:T(1024)}), (f32[2359296]{0:T(1024)}, f32[262144]{0:T(1024)})) %all-reduce.8.cloned.1.call-update) | async-done | bytes 10485776
  785.4 1.4 dynamic-slice
  (146 shorter events, 34.4 us)
Async XLA Ops:
  7.2 58.9 %copy-start = (bf16[512,1536]{1,0:T(8,128)(2,1)S(1)}, bf16[512,1536]{1,0:T(8,128)(2,1)}, u32[]{:S(2)}) copy-start(bf16[512,1536]{1,0:T(8,128)(2,1)} %param.14) | copy-start | bytes 4718596
  7.2 61.2 %copy-start.4 = (bf16[1,4,64,512]{3,2,1,0:T(8,128)(2,1)S(1)}, bf16[1,4,64,512]{3,2,1,0:T(8,128)(2,1)}, u32[]{:S(2)}) copy-start(bf16[1,4,64,512]{3,2,1,0:T(8,128)(2,1)} %param.17) | copy-start | bytes 786436
  7.2 67.5 %copy-start.8 = (bf16[128,512]{1,0:T(8,128)(2,1)S(1)}, bf16[128,512]{1,0:T(8,128)(2,1)}, u32[]{:S(2)}) copy-start(bf16[128,512]{1,0:T(8,128)(2,1)} %param.12) | copy-start | bytes 393220
  7.2 170.2 %all-gather.3.cloned.1.call-start = ((), (), s32[]{:S(2)}) async-start(), calls=%async_computation | async-start | bytes 4456448 | tf_op jit(solution)/shard_map/all_gather | solution.py:129
  67.5 211.1 %all-gather.5.cloned.1.call-start = ((), (), s32[]{:S(2)}) async-start(), calls=%async_computation.1 | async-start | bytes 4456448 | tf_op jit(solution)/shard_map/all_gather | solution.py:130
  68.3 717.1 %all-reduce.8.cloned.1.call-start = ((), (), s32[]{:S(2)}) async-start(), calls=%async_computation.2 | async-start | bytes 20971520
  68.4 8.5 %collective-permute-start.3 = (bf16[1,1,64,512]{3,2,1,0:T(8,128)(2,1)S(1)}, bf16[1,1,64,512]{3,2,1,0:T(8,128)(2,1)S(1)}, u32[]{:S(2)}, u32[]{:S(2)}) collective-permute-start(bf16[1,1,64,512]{3,2,1,0:T(8,128)(2,1)S(1)} %get-tuple-element.117), channel_id=1, source_target_pairs={{1,0},{2,1},{3,2},{4,3},{5,4},{6,5},{7,6},{8,7},{9,8},{10,9},{11,1... | collective-permute-start | bytes 196616 | tf_op jit(solution)/shard_map/ppermute | solution.py:26
  69.7 7.2 collective-permute-start.2
  76.8 5.2 copy-start.3
  299.5 73.9 %copy-start.6 = (bf16[1,4,64,512]{3,2,1,0:T(8,128)(2,1)S(1)}, bf16[1,4,64,512]{3,2,1,0:T(8,128)(2,1)}, u32[]{:S(2)}) copy-start(bf16[1,4,64,512]{3,2,1,0:T(8,128)(2,1)} %param.10) | copy-start | bytes 786436
  303.3 3.4 copy-start.2
  312.5 3.4 copy-start.2
  321.6 3.4 copy-start.2
  330.8 3.4 copy-start.2
  340.0 3.4 copy-start.2
  349.2 3.4 copy-start.2
  358.4 3.4 copy-start.2
  367.6 3.4 copy-start.2
  454.1 8.2 %copy-start.7 = (bf16[1,4,64,512]{3,2,1,0:T(8,128)(2,1)}, bf16[1,4,64,512]{3,2,1,0:T(8,128)(2,1)S(1)}, u32[]{:S(2)}) copy-start(bf16[1,4,64,512]{3,2,1,0:T(8,128)(2,1)S(1)} %get-tuple-element.114) | copy-start | bytes 786436
  454.1 7.0 collective-permute-start.1
  455.4 5.7 collective-permute-start
  464.2 3.7 copy-start.5
  481.7 306.3 %copy-start.1 = (bf16[512,1536]{1,0:T(8,128)(2,1)S(1)}, bf16[512,1536]{1,0:T(8,128)(2,1)}, u32[]{:S(2)}) copy-start(bf16[512,1536]{1,0:T(8,128)(2,1)} %param.14) | copy-start | bytes 4718596
Sparse Core Ops, SparseCore 0:
  67.7 109.7 all-gather.2
  179.8 98.7 all-gather.4
  477.8 307.5 all-reduce.7
where the time goes:
time: 798 us; the launch traced here: 795 us
  waiting for transfers between devices  469 us (59%)
  blocking collectives  131 us (16%)
  matrix products  74.3 us (9%)
  local copies, waits for them, and re-layouts  64.8 us (8%)
  other arithmetic  29.2 us (4%)
  between operations  14.8 us (2%)
  starting transfers between devices  11.2 us (1%)
    unnamed x4, waiting for transfers between devices  295 us
    psum x4, blocking collectives, single_sum(): return lax.psum(partial_value, 'space')  106 us
    all_gather x1, waiting for transfers between devices, on_device(): lax.all_gather(projected[..., width:2 * width], 'space', axis=1, tiled=True)  93.6 us
    all_gather x1, waiting for transfers between devices, on_device(): lax.all_gather(projected[..., 2 * width:], 'space', axis=1, tiled=True)  80.3 us
    unnamed x22, local copies, waits for them, and re-layouts  36.8 us
    dot_general x8, matrix products, advance(): jnp.einsum('iqhd,ikhd->ihqk', queries, key_block, preferred_element_type=...  29.9 us
    psum x1, blocking collectives, pair_sums(): return lax.psum((first, second), 'space')  24.8 us
    reduce_sum x8, other arithmetic, advance(): running_total = running_total * shrink + jnp.sum(weights, axis=3)  24.3 us
  transfers between devices with their start and end apart: 7, of which 3 were waited for; matrix products, arithmetic and copies ran while one was open for 6% of the time, Pallas kernels for 0%

commit v1 on v0

v1 whole, which is shorter than its diff:
```python
import functools
import math

import jax
import jax.numpy as jnp
from jax import lax
from jax.experimental import pallas as pl
from jax.experimental.pallas import tpu as pltpu
from jax.sharding import PartitionSpec as P

MESH = pl.DeviceIdType.MESH
F32 = jnp.float32
BF16 = jnp.bfloat16
EPS = 1e-05
LOG2E = 1.4426950408889634
TFEAT = 128
N = 16
CELLS = 256
W = 512
NEAR = (0, 1, 7, 2, 6, 3, 5, 4)
FAR = (4, 3, 5, 2, 6, 1, 7)


def rcopy(src, dst, ssem, rsem, dev):
    return pltpu.make_async_remote_copy(
        src_ref=src, dst_ref=dst, send_sem=ssem, recv_sem=rsem, device_id=dev, device_id_type=MESH
    )


def loop(lo, hi, fn):
    def body(k, carry):
        fn(k)
        return carry

    lax.fori_loop(lo, hi, body, 0)


def share_start(buf, ssem, rsem, s):
    def go(k):
        t = lax.rem(s + k, N)
        rcopy(buf.at[s], buf.at[s], ssem.at[k], rsem.at[s], {"space": t}).start()

    loop(1, N, go)


def share_wait(buf, ssem, rsem, s):
    def go(k):
        t = lax.rem(s + k, N)
        copy = rcopy(buf.at[t], buf.at[t], ssem.at[k], rsem.at[t], {"space": t})
        copy.wait_send()
        copy.wait_recv()

    loop(1, N, go)


def group_sum(v):
    lane = lax.broadcasted_iota(jnp.int32, v.shape, 1)
    for k in (1, 2, 4, 8):
        v = v + jnp.where((lane & k) == 0, pltpu.roll(v, 128 - k, 1), pltpu.roll(v, k, 1))
    return v


def pack(a, b):
    return jnp.concatenate(
        [a[:, 128 * q : 128 * q + 128] for q in range(4)]
        + [b[:, 128 * q : 128 * q + 128] for q in range(4)],
        axis=0,
    )


def unpack(v, first=0):
    return jnp.concatenate([v[first + q : first + q + 1, :] for q in range(4)], axis=1)


def local_moments(values):
    mu = jnp.sum(values, axis=0, keepdims=True) / CELLS
    off = values - mu
    return pack(mu, jnp.sum(off * off, axis=0, keepdims=True))


def moments(buf):
    every = buf[...]
    total = jnp.sum(every, axis=0)
    mean = group_sum(total) / 256.0
    off = every - mean[None]
    spread = jnp.sum(off * off, axis=0) * CELLS + pltpu.roll(total, 4, 0)
    inverse = lax.rsqrt(group_sum(spread) / 65536.0 + EPS)
    return unpack(mean), unpack(inverse)


def dot(a, b):
    return jnp.dot(a, b, preferred_element_type=F32)


def dot_nt(a, b):
    return lax.dot_general(a, b, (((1,), (1,)), ((), ())), preferred_element_type=F32)


def exact_dot(v, w):
    high = v.astype(BF16)
    rest = v - high.astype(F32)
    mid = rest.astype(BF16)
    low = (rest - mid.astype(F32)).astype(BF16)
    return dot(high, w) + dot(mid, w) + dot(low, w)


def windows(v, dst):
    col = lax.broadcasted_iota(jnp.int32, v.shape, 0) & 63
    height = v.shape[0]
    dst[:, 0:W] = jnp.where(col != 0, pltpu.roll(v, 1, 0), 0.0).astype(BF16)
    dst[:, W : 2 * W] = v.astype(BF16)
    dst[:, 2 * W : 3 * W] = jnp.where(col != 63, pltpu.roll(v, height - 1, 0), 0.0).astype(BF16)


def silu(v):
    return v * jax.nn.sigmoid(v)


def kernel(
    x_ref, tf_ref, up_hbm, wtime_hbm, wemb_hbm, wqkv_hbm, wout_hbm, wconv_hbm,
    out_ref, gf_ref, gc_ref, go_ref,
    wtime, wemb, wqkv, wout, wconv,
    st1, st2, st3,
    kvs, qs, kvr, qr, val, score, prob, ats, atr, att,
    upp, pupp, umat, pumat, actp, amat, pact, patt, pgf, actt, attt,
    hat, zed, back, thr, mod,
    gst, grecv, gost, gorecv, sum2, piece32, piece, precv, opiece, oprecv,
    lsem,
    st_ssem, st_rsem,
    kv_ssem, kv_rsem, fw_ssem, q_ssem, q_rsem, at_ssem, at_rsem,
    halo_ssem, halo_rsem, pair_ssem, pair_rsem,
    g_ssem, g_rsem, o_ssem, o_rsem, p_ssem, p_rsem, op_ssem, op_rsem,
):
    d = lax.axis_index("dp")
    s = lax.axis_index("space")
    z = s // 2
    xl = lax.rem(s, 2)
    chip = d // 2
    core = lax.rem(d, 2)
    mate = {"dp": 2 * chip + 1 - core, "space": s}

    loads = [
        pltpu.make_async_copy(a, b, lsem.at[i])
        for i, (a, b) in enumerate(
            (
                (wqkv_hbm, wqkv),
                (up_hbm, upp.at[pl.ds(64, CELLS)]),
                (wtime_hbm, wtime),
                (wemb_hbm, wemb),
                (wconv_hbm, wconv),
                (wout_hbm, wout),
            )
        )
    ]
    for load in loads:
        load.start()

    blank = jnp.zeros((64, W), BF16)
    for ref in (upp, actp):
        ref[0:64, :] = blank
        ref[320:384, :] = blank

    barrier = pltpu.get_barrier_semaphore()

    def greet_space(k):
        pl.semaphore_signal(
            barrier, inc=1, device_id={"space": lax.rem(s + k, N)}, device_id_type=MESH
        )

    def greet_other_core(k):
        pl.semaphore_signal(
            barrier, inc=1, device_id={"dp": 2 * chip + 1 - core}, device_id_type=MESH
        )

    def greet_chips(k):
        pl.semaphore_signal(
            barrier,
            inc=1,
            device_id={"dp": 2 * lax.rem(chip + k, 8) + core},
            device_id_type=MESH,
        )

    loop(1, N, greet_space)
    loop(0, 1, greet_other_core)
    loop(1, 8, greet_chips)

    st1[s] = local_moments(x_ref[...].astype(F32))
    pl.semaphore_wait(barrier, 15 + 1 + 7)
    share_start(st1, st_ssem.at[0], st_rsem.at[0], s)

    loads[1].wait()
    up_top = rcopy(
        upp.at[pl.ds(64, 64)], upp.at[pl.ds(320, 64)], halo_ssem.at[0], halo_rsem.at[0],
        {"space": jnp.maximum(s - 1, 0)},
    )
    up_bottom = rcopy(
        upp.at[pl.ds(256, 64)], upp.at[pl.ds(0, 64)], halo_ssem.at[1], halo_rsem.at[1],
        {"space": jnp.minimum(s + 1, N - 1)},
    )

    @pl.when(s > 0)
    def _():
        up_top.start()

    @pl.when(s < N - 1)
    def _():
        up_bottom.start()

    share_wait(st1, st_ssem.at[0], st_rsem.at[0], s)
    mean1, inverse1 = moments(st1)
    normed = ((x_ref[...].astype(F32) - mean1) * inverse1).astype(BF16)
    loads[0].wait()
    low_half = lax.broadcasted_iota(jnp.int32, (CELLS, 128), 1) < 64
    low_short = lax.broadcasted_iota(jnp.int32, (128, 128), 1) < 64
    for pair in range(4):
        cols = [dot(normed, wqkv[:, W * j + 128 * pair : W * j + 128 * pair + 128]) for j in range(3)]
        q, k, v = cols
        q = q.astype(BF16).astype(F32) * 0.125
        turned_q = pltpu.roll(q, 64, 1)
        qs[2 * pair] = jnp.where(low_short, q[0:128], turned_q[128:256]).astype(BF16)
        qs[2 * pair + 1] = jnp.where(low_short, turned_q[0:128], q[128:256]).astype(BF16)
        kvs[2 * pair] = jnp.where(low_half, k, pltpu.roll(v, 64, 1)).astype(BF16)
        kvs[2 * pair + 1] = jnp.where(low_half, pltpu.roll(k, 64, 1), v).astype(BF16)

    for k in FAR:
        h = lax.rem(z + k, 8)
        dev = {"space": 2 * h + xl}
        rcopy(kvs.at[h], kvr.at[s], kv_ssem.at[k], kv_rsem.at[s], dev).start()
        rcopy(qs.at[h], qr.at[z], q_ssem.at[k], q_rsem.at[z], dev).start()
    kvr[s] = kvs[z]
    qr[z] = qs[z]

    loads[2].wait()
    loads[3].wait()
    embedded = exact_dot(tf_ref[...], wtime[...])
    mod[...] = exact_dot(silu(embedded), wemb[...])

    @pl.when(s < N - 1)
    def _():
        up_top.wait_recv()

    @pl.when(s > 0)
    def _():
        up_bottom.wait_recv()

    pair_up = rcopy(upp, pupp, pair_ssem.at[0], pair_rsem.at[0], mate)
    pair_up.start()
    windows(upp[...].astype(F32), umat)
    loads[4].wait()
    loads[5].wait()
    back[...] = jnp.zeros_like(back)

    def back_step(p):
        a = p // 3
        b = lax.rem(p, 3)
        rows = pl.ds(pl.multiple_of(64 * (2 - a), 64), CELLS)
        lanes = pl.ds(pl.multiple_of(W * (2 - b), W), W)
        back[...] += dot_nt(umat[rows, lanes], wconv[pl.ds(pl.multiple_of(W * p, W), W), :])

    loop(0, 9, back_step)
    pair_up.wait_recv()
    windows(pupp[...].astype(F32), pumat)

    other = {"space": 2 * z + 1 - xl}
    for k in NEAR:
        zz = lax.rem(z + k, 8)
        mine = 2 * zz + xl
        if k:
            rcopy(kvs.at[zz], kvr.at[mine], kv_ssem.at[k], kv_rsem.at[mine], other).wait_recv()
        rcopy(kvr.at[mine], kvr.at[mine], fw_ssem.at[k], kv_rsem.at[mine], other).start()
    for k in NEAR:
        zz = lax.rem(z + k, 8)
        if k:
            rcopy(qs.at[zz], qr.at[zz], q_ssem.at[k], q_rsem.at[zz], other).wait_recv()
    for k in NEAR:
        theirs = 2 * lax.rem(z + k, 8) + 1 - xl
        rcopy(kvr.at[theirs], kvr.at[theirs], fw_ssem.at[k], kv_rsem.at[theirs], other).wait_recv()

    def make_values(j):
        val[pl.ds(pl.multiple_of(CELLS * j, CELLS), CELLS), :] = jnp.where(
            low_half, 1.0, kvr[j].astype(F32)
        ).astype(BF16)

    loop(0, N, make_values)

    def attend(zz):
        q = qr[zz].astype(F32)
        qq = jnp.concatenate(
            [jnp.where(low_short, q, 0.0), jnp.where(low_short, pltpu.roll(q, 64, 1), 0.0)], axis=0
        ).astype(BF16)
        top = jnp.full((CELLS, 128), -jnp.inf, F32)
        for j in range(N):
            part = dot_nt(qq, kvr[j])
            score[:, CELLS * j : CELLS * j + CELLS] = part
            top = jnp.maximum(top, jnp.maximum(part[:, 0:128], part[:, 128:256]))
        top = jnp.max(top, axis=1, keepdims=True) * LOG2E
        for j in range(N):
            at = slice(CELLS * j, CELLS * j + CELLS)
            prob[:, at] = jnp.exp2(score[:, at] * LOG2E - top).astype(BF16)
        mixed = dot(prob[...], val[...])
        ratio = mixed / pltpu.roll(mixed, 64, 1)
        return jnp.where(low_short, pltpu.roll(ratio[0:128], 64, 1), ratio[128:256]).astype(BF16)

    def attend_far(k):
        zz = lax.rem(z + k, 8)
        ats[zz] = attend(zz)
        rcopy(
            ats.at[zz], atr.at[z], at_ssem.at[k], at_rsem.at[z], {"space": 2 * zz + xl}
        ).start()

    loop(1, 8, attend_far)
    atr[z] = attend(z)

    for k in NEAR[1:]:
        h = lax.rem(z + k, 8)
        rcopy(ats.at[h], atr.at[h], at_ssem.at[k], at_rsem.at[h], other).wait_recv()
    for pair in range(4):
        first = atr[2 * pair].astype(F32)
        second = atr[2 * pair + 1].astype(F32)
        lanes = slice(128 * pair, 128 * pair + 128)
        att[0:128, lanes] = jnp.where(low_short, first, pltpu.roll(second, 64, 1)).astype(BF16)
        att[128:256, lanes] = jnp.where(low_short, pltpu.roll(first, 64, 1), second).astype(BF16)
    pair_att = rcopy(att, patt, pair_ssem.at[1], pair_rsem.at[1], mate)
    pair_att.start()

    hidden = (x_ref[...].astype(F32) + dot(att[...], wout[...])).astype(BF16).astype(F32)
    st2[s] = local_moments(hidden)
    share_start(st2, st_ssem.at[1], st_rsem.at[1], s)
    thr[...] = hidden
    share_wait(st2, st_ssem.at[1], st_rsem.at[1], s)
    mean2, inverse2 = moments(st2)
    scale = 1.0 + mod[0:1, 0:W]
    shift = mod[0:1, W : 2 * W]
    hats = (thr[...] - mean2) * inverse2
    hat[...] = hats
    shifted = hats * scale + shift
    zed[...] = shifted
    actp[64:320, :] = silu(shifted).astype(BF16)

    act_top = rcopy(
        actp.at[pl.ds(64, 64)], actp.at[pl.ds(320, 64)], halo_ssem.at[2], halo_rsem.at[2],
        {"space": jnp.maximum(s - 1, 0)},
    )
    act_bottom = rcopy(
        actp.at[pl.ds(256, 64)], actp.at[pl.ds(0, 64)], halo_ssem.at[3], halo_rsem.at[3],
        {"space": jnp.minimum(s + 1, N - 1)},
    )

    @pl.when(s > 0)
    def _():
        act_top.start()

    @pl.when(s < N - 1)
    def _():
        act_bottom.start()

    pair_act = rcopy(actp.at[pl.ds(64, CELLS)], pact, pair_ssem.at[2], pair_rsem.at[2], mate)
    pair_act.start()

    sigma = jax.nn.sigmoid(zed[...])
    through = back[...] * sigma * (1.0 + zed[...] * (1.0 - sigma)) * scale
    thr[...] = through
    st3[s] = pack(
        jnp.sum(through, axis=0, keepdims=True),
        jnp.sum(through * hat[...], axis=0, keepdims=True),
    )
    share_start(st3, st_ssem.at[2], st_rsem.at[2], s)

    actt[:, 0:CELLS] = actp[64:320, :].T
    pair_act.wait_recv()
    actt[:, CELLS : 2 * CELLS] = pact[...].T

    def grad_step(j):
        p = lax.rem(chip + 1 + j, 9)
        a = p // 3
        b = lax.rem(p, 3)
        rows = pl.ds(pl.multiple_of(64 * (2 - a), 64), CELLS)
        lanes = pl.ds(pl.multiple_of(W * (2 - b), W), W)
        part = dot(actt[:, 0:CELLS], umat[rows, lanes]) + dot(
            actt[:, CELLS : 2 * CELLS], pumat[rows, lanes]
        )
        gst[pl.ds(pl.multiple_of(W * p, W), W), :] = part.astype(BF16)

        @pl.when((j >= 1) & (p >= 1))
        def _():
            to = p - 1
            rcopy(
                gst.at[pl.ds(pl.multiple_of(576 * to + 288 * core, 32), 288)],
                grecv.at[chip],
                g_ssem.at[to],
                g_rsem.at[chip],
                {"dp": 2 * to + core},
            ).start()

    loop(0, 9, grad_step)

    share_wait(st3, st_ssem.at[2], st_rsem.at[2], s)
    sums = group_sum(jnp.sum(st3[...], axis=0)) / 65536.0
    gf = (inverse2 * (thr[...] - unpack(sums) - hat[...] * unpack(sums, 4))).astype(BF16)
    gf_ref[...] = gf
    pair_gf = rcopy(gf_ref, pgf, pair_ssem.at[3], pair_rsem.at[3], mate)
    pair_gf.start()
    pair_att.wait_recv()
    attt[:, 0:CELLS] = att[...].T
    attt[:, CELLS : 2 * CELLS] = patt[...].T
    pair_gf.wait_recv()
    gost[...] = (
        dot(attt[:, 0:CELLS], gf_ref[...]) + dot(attt[:, CELLS : 2 * CELLS], pgf[...])
    ).astype(BF16)

    def send_out(k):
        to = lax.rem(chip + k, 8)
        rcopy(
            gost.at[pl.ds(pl.multiple_of(64 * to + 32 * core, 32), 32)],
            gorecv.at[chip],
            o_ssem.at[to],
            o_rsem.at[chip],
            {"dp": 2 * to + core},
        ).start()

    loop(1, 8, send_out)

    @pl.when(s < N - 1)
    def _():
        act_top.wait_recv()

    @pl.when(s > 0)
    def _():
        act_bottom.wait_recv()

    windows(actp[...].astype(F32), amat)
    thr[...] = jnp.zeros_like(thr)

    def conv_step(a):
        thr[...] += dot(
            amat[pl.ds(pl.multiple_of(64 * a, 64), CELLS), :],
            wconv[pl.ds(pl.multiple_of(3 * W * a, W), 3 * W), :],
        )

    loop(0, 3, conv_step)
    out_ref[...] = thr[...].astype(BF16)

    def take_out(k):
        frm = lax.rem(chip + k, 8)
        rcopy(gorecv.at[frm], gorecv.at[frm], o_ssem.at[frm], o_rsem.at[frm], mate).wait_recv()

    loop(1, 8, take_out)
    gorecv[chip] = gost[pl.ds(pl.multiple_of(64 * chip + 32 * core, 32), 32), :]
    out_sum = jnp.sum(gorecv[...].astype(F32), axis=0)
    for t in range(N):
        rows = out_sum[2 * t : 2 * t + 2]
        opiece[t] = pack(rows[0:1], rows[1:2])

    def send_opiece(k):
        t = lax.rem(s + k, N)
        rcopy(opiece.at[t], oprecv.at[s], op_ssem.at[k], op_rsem.at[s], {"space": t}).start()

    loop(1, N, send_opiece)
    oprecv[s] = opiece[s]

    def take_grad(k):
        frm = lax.rem(chip + k, 8)
        rcopy(grecv.at[frm], grecv.at[frm], g_ssem.at[frm], g_rsem.at[frm], mate).wait_recv()

    loop(1, 8, take_grad)
    grecv[chip] = gst[pl.ds(pl.multiple_of(576 * chip + 288 * core, 32), 288), :]
    sum2[...] = jnp.zeros_like(sum2)

    def add_grad(k):
        sum2[...] += grecv[k].astype(F32)

    loop(0, 8, add_grad)
    for t in range(N):
        for q in range(4):
            piece32[18 * q : 18 * q + 18, :] = sum2[18 * t : 18 * t + 18, 128 * q : 128 * q + 128]
        piece32[72:80, :] = jnp.zeros((8, 128), F32)
        piece[t] = piece32[...].astype(BF16)

    def send_piece(k):
        t = lax.rem(s + k, N)
        rcopy(piece.at[t], precv.at[s], p_ssem.at[k], p_rsem.at[s], {"space": t}).start()

    loop(1, N, send_piece)
    precv[s] = piece[s]

    def take_pieces(k):
        t = lax.rem(s + k, N)
        o = rcopy(opiece.at[t], oprecv.at[t], op_ssem.at[k], op_rsem.at[t], {"space": t})
        o.wait_send()
        o.wait_recv()
        g = rcopy(piece.at[t], precv.at[t], p_ssem.at[k], p_rsem.at[t], {"space": t})
        g.wait_send()
        g.wait_recv()

    loop(1, N, take_pieces)
    owned_out = jnp.sum(oprecv[...], axis=0)
    go_ref[...] = jnp.concatenate([unpack(owned_out), unpack(owned_out, 4)], axis=0)
    piece32[...] = jnp.sum(precv[...].astype(F32), axis=0)
    for q in range(4):
        gc_ref[:, 128 * q : 128 * q + 128] = piece32[18 * q : 18 * q + 18, :]

    for k in range(8):
        zz = lax.rem(z + k, 8)
        rcopy(kvr.at[0], kvr.at[0], fw_ssem.at[k], kv_rsem.at[0], other).wait_send()
        if k:
            rcopy(kvs.at[zz], kvr.at[0], kv_ssem.at[k], kv_rsem.at[0], other).wait_send()
            rcopy(qs.at[zz], qr.at[0], q_ssem.at[k], q_rsem.at[0], other).wait_send()
            rcopy(ats.at[zz], atr.at[0], at_ssem.at[k], at_rsem.at[0], other).wait_send()

    def chips_sent(k):
        to = lax.rem(chip + k, 8)
        rcopy(gorecv.at[to], gorecv.at[to], o_ssem.at[to], o_rsem.at[to], mate).wait_send()
        rcopy(grecv.at[to], grecv.at[to], g_ssem.at[to], g_rsem.at[to], mate).wait_send()

    loop(1, 8, chips_sent)
    for copy in (pair_up, pair_att, pair_act, pair_gf):
        copy.wait_send()

    @pl.when(s > 0)
    def _():
        up_top.wait_send()
        act_top.wait_send()

    @pl.when(s < N - 1)
    def _():
        up_bottom.wait_send()
        act_bottom.wait_send()


def time_features(timestep):
    halfway = TFEAT // 2
    frequency = jnp.exp(-math.log(10000.0) * jnp.arange(halfway, dtype=F32) / halfway)
    angles = timestep.astype(F32)[:, None] * frequency[None, :]
    return jnp.concatenate([jnp.cos(angles), jnp.sin(angles)], axis=1)


def on_device(features, timestep, w_time, w_emb, w_qkv, w_out, w_conv, upstream):
    tfeat = jnp.broadcast_to(time_features(timestep), (8, TFEAT))
    vmem = pl.BlockSpec(memory_space=pltpu.VMEM)
    hbm = pl.BlockSpec(memory_space=pl.ANY)
    V = pltpu.VMEM
    dma = pltpu.SemaphoreType.DMA
    scratch = [
        V((TFEAT, W), BF16), V((W, 2 * W), BF16), V((W, 3 * W), BF16), V((W, W), BF16), V((9 * W, W), BF16),
        V((N, 8, 128), F32), V((N, 8, 128), F32), V((N, 8, 128), F32),
        V((8, CELLS, 128), BF16), V((8, 128, 128), BF16), V((N, CELLS, 128), BF16), V((8, 128, 128), BF16),
        V((N * CELLS, 128), BF16), V((CELLS, N * CELLS), F32), V((CELLS, N * CELLS), BF16),
        V((8, 128, 128), BF16), V((8, 128, 128), BF16), V((CELLS, W), BF16),
        V((384, W), BF16), V((384, W), BF16), V((384, 3 * W), BF16), V((384, 3 * W), BF16),
        V((384, W), BF16), V((384, 3 * W), BF16),
        V((CELLS, W), BF16), V((CELLS, W), BF16), V((CELLS, W), BF16),
        V((W, 2 * CELLS), BF16), V((W, 2 * CELLS), BF16),
        V((CELLS, W), F32), V((CELLS, W), F32), V((CELLS, W), F32), V((CELLS, W), F32), V((8, 2 * W), F32),
        V((9 * W, W), BF16), V((8, 288, W), BF16), V((W, W), BF16), V((8, 32, W), BF16),
        V((288, W), F32), V((80, 128), F32), V((N, 80, 128), BF16), V((N, 80, 128), BF16),
        V((N, 8, 128), F32), V((N, 8, 128), F32),
        dma((6,)),
        dma((3, N)), dma((3, N)),
        dma((8,)), dma((N,)), dma((8,)), dma((8,)), dma((8,)), dma((8,)), dma((8,)),
        dma((4,)), dma((4,)), dma((4,)), dma((4,)),
        dma((8,)), dma((8,)), dma((8,)), dma((8,)), dma((N,)), dma((N,)), dma((N,)), dma((N,)),
    ]
    out, gf, gc, go = pl.pallas_call(
        kernel,
        out_shape=(
            jax.ShapeDtypeStruct((CELLS, W), BF16),
            jax.ShapeDtypeStruct((CELLS, W), BF16),
            jax.ShapeDtypeStruct((18, W), F32),
            jax.ShapeDtypeStruct((2, W), F32),
        ),
        in_specs=[vmem, vmem, hbm, hbm, hbm, hbm, hbm, hbm],
        out_specs=(vmem, vmem, vmem, vmem),
        scratch_shapes=scratch,
        compiler_params=pltpu.CompilerParams(
            collective_id=0, has_side_effects=True, vmem_limit_bytes=60 * 1024 * 1024
        ),
    )(
        features.reshape(CELLS, W), tfeat, upstream.reshape(CELLS, W),
        w_time, w_emb, w_qkv, w_out, w_conv,
    )
    return (
        out.reshape(features.shape),
        gf.reshape(features.shape),
        gc.reshape(-1),
        go.reshape(-1),
    )


def solution(mesh):
    return jax.shard_map(
        on_device,
        mesh=mesh,
        in_specs=(
            P("dp", "space", None, None), P("dp"), P(), P(), P(), P(), P(),
            P("dp", "space", None, None),
        ),
        out_specs=(
            P("dp", "space", None, None), P("dp", "space", None, None),
            P(("dp", "space")), P(("dp", "space")),
        ),
        check_vma=False,
    )
```

time: 798 us -> 130 us (0.16)
  waiting for transfers between devices: 469 us -> 0 us
  blocking collectives: 131 us -> 0 us
  Pallas kernels: 0 us -> 121 us
  matrix products: 74.3 us -> 0 us
  local copies, waits for them, and re-layouts: 64.8 us -> 6.63 us
  other arithmetic: 29.2 us -> 0.13 us
  between operations: 14.8 us -> 1.29 us
  starting transfers between devices: 11.2 us -> 0 us
    unnamed x4 -> x0, waiting for transfers between devices: 295 us -> none
    all_gather x2 -> x0, waiting for transfers between devices: 174 us -> none  [the longest x1 93.6 us: on_device(): lax.all_gather(projected[..., width:2 * width], 'space', axis=1, tiled=True)]
    psum x5 -> x0, blocking collectives: 131 us -> none  [the longest x4 106 us: single_sum(): return lax.psum(partial_value, 'space')]
    pallas_call x0 -> x1, Pallas kernels: none -> 121 us  [on_device(): pl.pallas_call(kernel, out_shape=(jax.ShapeDtypeStruct((CELLS, W), BF16),...]
    dot_general x48 -> x0, matrix products: 74.3 us -> none  [the longest x8 29.9 us: advance(): jnp.einsum('iqhd,ikhd->ihqk', queries, key_block, preferred_element_type=...]
    unnamed x22 -> x3, local copies, waits for them, and re-layouts: 36.8 us -> 4.6 us
    reduce_sum x18 -> x0, other arithmetic: 27.3 us -> none  [the longest x8 24.3 us: advance(): running_total = running_total * shrink + jnp.sum(weights, axis=3)]
    another operation x2 -> x0, local copies, waits for them, and re-layouts: 22.3 us -> none  [the longest x1 11.2 us: attend_blocks(): values.reshape(image_count, blocks, block, head_count, head_width)]
  transfers between devices with their start and end apart: 7 -> 0, of which waited for: 3 -> 0; matrix products, arithmetic and copies ran while one was open for 6% -> 0% of each run, Pallas kernels for 0% -> 0%
where the time goes in v1:
time: 130 us; the launch traced here: 129 us
  Pallas kernels  121 us (93%)
  local copies, waits for them, and re-layouts  6.63 us (5%)
    pallas_call x1, Pallas kernels, on_device(): pl.pallas_call(kernel, out_shape=(jax.ShapeDtypeStruct((CELLS, W), BF16),...  121 us
    unnamed x3, local copies, waits for them, and re-layouts  4.6 us

profile of v1, /device:TPU:1, one launch (start us, length us, event | category | flops | bytes accessed | tf_op | source)
XLA Modules:
  0.0 129.5 jit_solution(13555056165997797770)
XLA Ops:
  1.3 0.1 fusion
  1.3 0.1 maximum_bitcast_fusion
  1.4 0.6 broadcast_in_dim.10.tf_ref
  2.0 121.4 %shard_map.111 = (bf16[256,512]{1,0:T(8,128)(2,1)}, bf16[256,512]{1,0:T(8,128)(2,1)}, f32[18,512]{1,0:T(8,128)}, f32[2,512]{1,0:T(2,128)}) custom-call(bf16[256,512]{1,0:T(8,128)(2,1)} %bitcast.11, f32[8,128]{1,0:T(8,128)} %broadcast_in_dim.10.tf_ref, bf16[256,512]{1,0:T(8,128)(2,1)} %bitcast.12, bf16[128,512]{1,0:T(8,128)(2,1)} %wtime_hbm.1, ...), custom_call_target="tpu_custom_call" | custom-call | tf_op jit(solution)/shard_map/pallas_call | solution.py:563
  123.5 1.3 copy.12
  124.7 1.4 %reshape.56 = f32[9216]{0:T(1024)} reshape(f32[18,512]{1,0:T(8,128)} %get-tuple-element.10) | data formatting | bytes 73728 | tf_op jit(solution)/shard_map/reshape | solution.py:584
  126.1 1.7 %copy.16 = bf16[1,4,64,512]{3,2,1,0:T(8,128)(2,1)} copy(bf16[1,4,64,512]{3,2,1,0:T(8,128)(2,1)} %bitcast.10) | data formatting | bytes 524288
  127.8 1.7 %copy.17 = bf16[1,4,64,512]{3,2,1,0:T(8,128)(2,1)} copy(bf16[1,4,64,512]{3,2,1,0:T(8,128)(2,1)} %bitcast.9) | data formatting | bytes 524288

commit v2 on v1

v2 whole, which is shorter than its diff:
```python
import functools
import math

import jax
import jax.numpy as jnp
from jax import lax
from jax.experimental import pallas as pl
from jax.experimental.pallas import tpu as pltpu
from jax.sharding import PartitionSpec as P

MESH = pl.DeviceIdType.MESH
F32 = jnp.float32
BF16 = jnp.bfloat16
EPS = 1e-05
LOG2E = 1.4426950408889634
TFEAT = 128
N = 16
CELLS = 256
W = 512
HALF = 256
NEAR = (0, 1, 7, 2, 6, 3, 5, 4)


def rcopy(src, dst, ssem, rsem, dev):
    return pltpu.make_async_remote_copy(
        src_ref=src, dst_ref=dst, send_sem=ssem, recv_sem=rsem, device_id=dev, device_id_type=MESH
    )


def loop(lo, hi, fn):
    def body(k, carry):
        fn(k)
        return carry

    lax.fori_loop(lo, hi, body, 0)


def share_start(buf, ssem, rsem, s):
    def go(k):
        t = lax.rem(s + k, N)
        rcopy(buf.at[s], buf.at[s], ssem.at[k], rsem.at[s], {"space": t}).start()

    loop(1, N, go)


def share_wait(buf, ssem, rsem, s):
    def go(k):
        t = lax.rem(s + k, N)
        copy = rcopy(buf.at[t], buf.at[t], ssem.at[k], rsem.at[t], {"space": t})
        copy.wait_send()
        copy.wait_recv()

    loop(1, N, go)


def group_sum(v):
    lane = lax.broadcasted_iota(jnp.int32, v.shape, 1)
    for k in (1, 2, 4, 8):
        v = v + jnp.where((lane & k) == 0, pltpu.roll(v, 128 - k, 1), pltpu.roll(v, k, 1))
    return v


def pack(a, b):
    return jnp.concatenate(
        [a[:, 128 * q : 128 * q + 128] for q in range(4)]
        + [b[:, 128 * q : 128 * q + 128] for q in range(4)],
        axis=0,
    )


def unpack(v, first=0):
    return jnp.concatenate([v[first + q : first + q + 1, :] for q in range(4)], axis=1)


def local_moments(values):
    mu = jnp.sum(values, axis=0, keepdims=True) / CELLS
    off = values - mu
    return pack(mu, jnp.sum(off * off, axis=0, keepdims=True))


def moments(buf):
    every = buf[...]
    total = jnp.sum(every, axis=0)
    mean = group_sum(total) / 256.0
    off = every - mean[None]
    spread = jnp.sum(off * off, axis=0) * CELLS + pltpu.roll(total, 4, 0)
    inverse = lax.rsqrt(group_sum(spread) / 65536.0 + EPS)
    return unpack(mean), unpack(inverse)


def dot(a, b):
    return jnp.dot(a, b, preferred_element_type=F32)


def dot_nt(a, b):
    return lax.dot_general(a, b, (((1,), (1,)), ((), ())), preferred_element_type=F32)


def exact_dot(v, w):
    high = v.astype(BF16)
    rest = v - high.astype(F32)
    mid = rest.astype(BF16)
    low = (rest - mid.astype(F32)).astype(BF16)
    return dot(high, w) + dot(mid, w) + dot(low, w)


def windows(v, dst):
    col = lax.broadcasted_iota(jnp.int32, v.shape, 0) & 63
    height, width = v.shape
    dst[:, 0:width] = jnp.where(col != 0, pltpu.roll(v, 1, 0), 0.0).astype(BF16)
    dst[:, width : 2 * width] = v.astype(BF16)
    dst[:, 2 * width : 3 * width] = jnp.where(col != 63, pltpu.roll(v, height - 1, 0), 0.0).astype(
        BF16
    )


def silu(v):
    return v * jax.nn.sigmoid(v)


def kernel(
    x_hbm, tf_ref, up_hbm, wtime_hbm, wemb_hbm, wqkv_hbm, wout_hbm, wconv_hbm,
    out_hbm, gf_hbm, gc_ref, go_ref,
    x_ref, wtime, wemb, wqkv, wout, wconv,
    st1, st2, st3,
    kvs, qs, kvr, qr, qq, val, top, acc, ats, atr, att,
    upp, uo, uh, umat, umat4,
    hid, hx, hfar, actp, xact, amat, patt, gf_ref, pgf, actt, attt,
    out_ref, hat, zed, back, thr, mod,
    gst, grecv, gost, gorecv, sum2, piece32, piece, precv, opiece, oprecv,
    lsem,
    st_ssem, st_rsem,
    kv_ssem, kv_rsem, fw_ssem, q_ssem, q_rsem, at_ssem, at_rsem,
    halo_ssem, halo_rsem, pair_ssem, pair_rsem,
    g_ssem, g_rsem, o_ssem, o_rsem, p_ssem, p_rsem, op_ssem, op_rsem,
):
    d = lax.axis_index("dp")
    s = lax.axis_index("space")
    z = s // 2
    xl = lax.rem(s, 2)
    chip = d // 2
    core = lax.rem(d, 2)
    mate = {"dp": 2 * chip + 1 - core}
    other = {"space": 2 * z + 1 - xl}

    barrier = pltpu.get_barrier_semaphore()

    def greet(dev):
        pl.semaphore_signal(barrier, inc=1, device_id=dev, device_id_type=MESH)

    loop(1, N, lambda k: greet({"space": lax.rem(s + k, N)}))
    loop(1, 8, lambda k: greet({"dp": 2 * lax.rem(chip + k, 8) + core}))
    greet(mate)

    loads = [
        pltpu.make_async_copy(a, b, lsem.at[i])
        for i, (a, b) in enumerate(
            (
                (x_hbm, x_ref),
                (wqkv_hbm, wqkv),
                (up_hbm, upp.at[pl.ds(64, CELLS)]),
                (wtime_hbm, wtime),
                (wemb_hbm, wemb),
                (wconv_hbm, wconv),
                (wout_hbm, wout),
            )
        )
    ]
    loads[0].start()
    loads[1].start()

    blank = jnp.zeros((64, W), BF16)

    @pl.when(s == 0)
    def _():
        upp[0:64, :] = blank

    @pl.when(s == N - 1)
    def _():
        upp[320:384, :] = blank

    loads[0].wait()
    st1[s] = local_moments(x_ref[...].astype(F32))
    for load in loads[2:]:
        load.start()
    pl.semaphore_wait(barrier, 15 + 7 + 1)
    share_start(st1, st_ssem.at[0], st_rsem.at[0], s)

    loads[2].wait()
    up_top = rcopy(
        upp.at[pl.ds(64, 64)], upp.at[pl.ds(320, 64)], halo_ssem.at[0], halo_rsem.at[0],
        {"space": jnp.maximum(s - 1, 0)},
    )
    up_bottom = rcopy(
        upp.at[pl.ds(256, 64)], upp.at[pl.ds(0, 64)], halo_ssem.at[1], halo_rsem.at[1],
        {"space": jnp.minimum(s + 1, N - 1)},
    )

    @pl.when(s > 0)
    def _():
        up_top.start()

    @pl.when(s < N - 1)
    def _():
        up_bottom.start()


    loads[1].wait()
    share_wait(st1, st_ssem.at[0], st_rsem.at[0], s)
    mean1, inverse1 = moments(st1)
    normed = ((x_ref[...].astype(F32) - mean1) * inverse1).astype(BF16)
    low_half = lax.broadcasted_iota(jnp.int32, (CELLS, 128), 1) < 64
    low_short = lax.broadcasted_iota(jnp.int32, (128, 128), 1) < 64
    for pair in range(4):
        q = dot(normed, wqkv[:, 128 * pair : 128 * pair + 128])
        q = q.astype(BF16).astype(F32) * 0.125
        turned = pltpu.roll(q, 64, 1)
        qs[2 * pair] = jnp.where(low_short, q[0:128], turned[128:256]).astype(BF16)
        qs[2 * pair + 1] = jnp.where(low_short, turned[0:128], q[128:256]).astype(BF16)

    def q_copy(p):
        h = lax.rem(z + NEAR[p], 8)
        slot = NEAR.index((8 - NEAR[p]) % 8)
        return rcopy(
            qs.at[h], qr.at[slot], q_ssem.at[p], q_rsem.at[slot], {"space": 2 * h + xl}
        )

    def kv_copy(p):
        h = lax.rem(z + NEAR[p], 8)
        slot = NEAR.index((8 - NEAR[p]) % 8)
        return rcopy(
            kvs.at[h], kvr.at[slot], kv_ssem.at[p], kv_rsem.at[slot], {"space": 2 * h + xl}
        )

    def forward(p):
        return rcopy(kvr.at[p], kvr.at[8 + p], fw_ssem.at[p], kv_rsem.at[8 + p], other)

    for p in range(1, 8):
        q_copy(p).start()
    for pair in range(4):
        k = dot(normed, wqkv[:, W + 128 * pair : W + 128 * pair + 128])
        v = dot(normed, wqkv[:, 2 * W + 128 * pair : 2 * W + 128 * pair + 128])
        kvs[2 * pair] = jnp.where(low_half, k, pltpu.roll(v, 64, 1)).astype(BF16)
        kvs[2 * pair + 1] = jnp.where(low_half, pltpu.roll(k, 64, 1), v).astype(BF16)
    for p in (1, 2):
        kv_copy(p).start()
    kvr[0] = kvs[z]
    qr[0] = qs[z]
    forward(0).start()

    loads[3].wait()
    loads[4].wait()
    embedded = exact_dot(tf_ref[...], wtime[...])
    mod[...] = exact_dot(silu(embedded), wemb[...])

    @pl.when(s < N - 1)
    def _():
        up_top.wait_recv()

    @pl.when(s > 0)
    def _():
        up_bottom.wait_recv()

    uh[0] = upp[:, pl.ds(pl.multiple_of(HALF * xl, HALF), HALF)]
    uo[...] = upp[:, pl.ds(pl.multiple_of(HALF * (1 - xl), HALF), HALF)]
    up_mate = rcopy(uh.at[0], uh.at[2], pair_ssem.at[0], pair_rsem.at[0], mate)
    up_other = rcopy(uo, uh.at[1], pair_ssem.at[1], pair_rsem.at[1], other)
    up_both = rcopy(uh.at[1], uh.at[3], pair_ssem.at[2], pair_rsem.at[2], mate)
    up_mate.start()
    up_other.start()
    windows(upp[...].astype(F32), umat)
    windows(uh[0].astype(F32), umat4.at[0])
    loads[5].wait()
    loads[6].wait()
    back[...] = jnp.zeros_like(back)

    def back_step(p):
        a = p // 3
        b = lax.rem(p, 3)
        rows = pl.ds(pl.multiple_of(64 * (2 - a), 64), CELLS)
        lanes = pl.ds(pl.multiple_of(W * (2 - b), W), W)
        back[...] += dot_nt(umat[rows, lanes], wconv[pl.ds(pl.multiple_of(W * p, W), W), :])

    loop(0, 9, back_step)

    for p in range(1, 8):
        q_copy(NEAR.index((8 - NEAR[p]) % 8)).wait_recv()
    kv_copy(3).start()
    kv_copy(4).start()
    for p in range(8):
        q = qr[p].astype(F32)
        qq[p, 0:128, :] = jnp.where(low_short, q, 0.0).astype(BF16)
        qq[p, 128:256, :] = jnp.where(low_short, pltpu.roll(q, 64, 1), 0.0).astype(BF16)

    def take(p):
        if 1 <= p < 8:
            kv_copy(NEAR.index((8 - NEAR[p]) % 8)).wait_recv()
            forward(p).start()
        if p >= 8:
            forward(p - 8).wait_recv()
        val[p] = jnp.where(low_half, 1.0, kvr[p].astype(F32)).astype(BF16)

    def attend(i, slots, first, last):
        query = qq[i]
        parts = [dot_nt(query, kvr[p]) for p in slots]
        high = None
        for part in parts:
            part = jnp.maximum(part[:, 0:128], part[:, 128:256])
            high = part if high is None else jnp.maximum(high, part)
        high = jnp.max(high, axis=1, keepdims=True) * LOG2E
        if not first:
            before = top[i]
            high = jnp.maximum(before, high)
        else:
            high = jnp.broadcast_to(high, (CELLS, 128))
        wide = jnp.concatenate([high, high], axis=1)
        total = None
        for part, p in zip(parts, slots):
            mixed = dot(jnp.exp2(part * LOG2E - wide).astype(BF16), val[p])
            total = mixed if total is None else total + mixed
        if not first:
            total = total + acc[i] * jnp.exp2(before - high)
        if last:
            return total
        top[i] = high
        acc[i] = total

    def finish(total):
        ratio = total / pltpu.roll(total, 64, 1)
        return jnp.where(low_short, pltpu.roll(ratio[0:128], 64, 1), ratio[128:256]).astype(BF16)

    def go(*slots):
        loop(0, 8, lambda i: attend(i, slots, 0 in slots, False))

    take(0)
    take(1)
    take(2)
    kv_copy(5).start()
    kv_copy(6).start()
    go(0, 1, 2)
    take(3)
    take(4)
    kv_copy(7).start()
    up_other.wait_recv()
    up_both.start()
    take(8)
    go(3, 4, 8)
    take(9)
    take(10)
    take(5)
    take(6)
    go(9, 10, 5, 6)
    take(7)
    take(11)
    take(12)
    go(7, 11, 12)
    for p in (13, 14, 15):
        take(p)

    def last_far(k):
        i = 8 - k
        zz = lax.rem(z + jnp.where(lax.rem(i, 2) == 1, (i + 1) // 2, 8 - i // 2), 8)
        ats[i] = finish(attend(i, (13, 14, 15), False, True))
        rcopy(
            ats.at[i], atr.at[z], at_ssem.at[i], at_rsem.at[z], {"space": 2 * zz + xl}
        ).start()

    loop(1, 8, last_far)
    atr[z] = finish(attend(0, (13, 14, 15), False, True))

    windows(uh[1].astype(F32), umat4.at[1])
    for k in range(1, 8):
        h = lax.rem(z + k, 8)
        rcopy(ats.at[k], atr.at[h], at_ssem.at[k], at_rsem.at[h], other).wait_recv()
    for pair in range(4):
        first = atr[2 * pair].astype(F32)
        second = atr[2 * pair + 1].astype(F32)
        lanes = slice(128 * pair, 128 * pair + 128)
        att[0:128, lanes] = jnp.where(low_short, first, pltpu.roll(second, 64, 1)).astype(BF16)
        att[128:256, lanes] = jnp.where(low_short, pltpu.roll(first, 64, 1), second).astype(BF16)

    hidden = (x_ref[...].astype(F32) + dot(att[...], wout[...])).astype(BF16)
    hid[...] = hidden
    hidden = hidden.astype(F32)
    st2[s] = local_moments(hidden)
    share_start(st2, st_ssem.at[1], st_rsem.at[1], s)
    far = s - 1 + 2 * xl
    has_far = (far >= 0) & (far < N)
    hid_far = rcopy(
        hid.at[pl.ds(pl.multiple_of(192 * xl, 64), 64)], hfar, halo_ssem.at[2], halo_rsem.at[2],
        {"space": jnp.clip(far, 0, N - 1)},
    )

    @pl.when(has_far)
    def _():
        hid_far.start()

    hid_other = rcopy(hid, hx, pair_ssem.at[3], pair_rsem.at[3], other)
    hid_other.start()
    pair_att = rcopy(att, patt, pair_ssem.at[4], pair_rsem.at[4], mate)
    pair_att.start()
    up_mate.wait_recv()
    windows(uh[2].astype(F32), umat4.at[2])
    up_both.wait_recv()
    windows(uh[3].astype(F32), umat4.at[3])
    attt[:, 0:CELLS] = att[...].T
    pair_att.wait_recv()
    attt[:, CELLS : 2 * CELLS] = patt[...].T

    share_wait(st2, st_ssem.at[1], st_rsem.at[1], s)
    mean2, inverse2 = moments(st2)
    scale = 1.0 + mod[0:1, 0:W]
    shift = mod[0:1, W : 2 * W]
    gain = inverse2 * scale

    def act_of(ref):
        return silu((ref[...].astype(F32) - mean2) * inverse2 * scale + shift).astype(BF16)

    hats = (hid[...].astype(F32) - mean2) * inverse2
    hat[...] = hats
    shifted = hats * scale + shift
    sigma = jax.nn.sigmoid(shifted)
    act = (shifted * sigma).astype(BF16)
    actp[64:320, :] = act
    actt[:, 0:CELLS] = act.T
    hid_other.wait_recv()
    xact[...] = act_of(hx)
    actt[:, CELLS : 2 * CELLS] = xact[...].T
    pair_act = rcopy(
        actt.at[:, pl.ds(0, 2 * CELLS)], actt.at[:, pl.ds(2 * CELLS, 2 * CELLS)],
        pair_ssem.at[5], pair_rsem.at[5], mate,
    )
    pair_act.start()

    through = back[...] * sigma * (1.0 + shifted * (1.0 - sigma)) * scale
    thr[...] = through
    st3[s] = pack(
        jnp.sum(through, axis=0, keepdims=True),
        jnp.sum(through * hats, axis=0, keepdims=True),
    )
    share_start(st3, st_ssem.at[2], st_rsem.at[2], s)

    actp[pl.ds(pl.multiple_of(320 * (1 - xl), 64), 64), :] = xact[
        pl.ds(pl.multiple_of(192 * xl, 64), 64), :
    ]
    edge = pl.ds(pl.multiple_of(320 * xl, 64), 64)

    @pl.when(has_far)
    def _():
        hid_far.wait_recv()
        actp[edge, :] = act_of(hfar)

    @pl.when(jnp.logical_not(has_far))
    def _():
        actp[edge, :] = blank

    windows(actp[...].astype(F32), amat)
    pair_act.wait_recv()

    def grad_step(j):
        p = lax.rem(chip + 1 + j, 9)
        a = p // 3
        b = lax.rem(p, 3)
        rows = pl.ds(pl.multiple_of(64 * (2 - a), 64), CELLS)
        lanes = pl.ds(pl.multiple_of(HALF * (2 - b), HALF), HALF)
        part = dot(actt[:, 0:CELLS], umat4[0, rows, lanes])
        for i in range(1, 4):
            part += dot(actt[:, CELLS * i : CELLS * i + CELLS], umat4[i, rows, lanes])
        gst[pl.ds(pl.multiple_of(W * p, W), W), :] = part.astype(BF16)

        @pl.when((j >= 1) & (p >= 1))
        def _():
            to = p - 1
            rcopy(
                gst.at[pl.ds(pl.multiple_of(576 * to + 288 * core, 32), 288)],
                grecv.at[chip],
                g_ssem.at[to],
                g_rsem.at[chip],
                {"dp": 2 * to + core},
            ).start()

    loop(0, 9, grad_step)

    share_wait(st3, st_ssem.at[2], st_rsem.at[2], s)
    sums = group_sum(jnp.sum(st3[...], axis=0)) / 65536.0
    gf_ref[...] = (inverse2 * (thr[...] - unpack(sums) - hat[...] * unpack(sums, 4))).astype(BF16)
    pair_gf = rcopy(gf_ref, pgf, pair_ssem.at[6], pair_rsem.at[6], mate)
    pair_gf.start()
    gf_out = pltpu.make_async_copy(gf_ref, gf_hbm, lsem.at[7])
    gf_out.start()
    part = dot(attt[:, 0:CELLS], gf_ref[...])
    pair_gf.wait_recv()
    gost[...] = (part + dot(attt[:, CELLS : 2 * CELLS], pgf[...])).astype(BF16)

    def send_out(k):
        to = lax.rem(chip + k, 8)
        rcopy(
            gost.at[pl.ds(pl.multiple_of(64 * to + 32 * core, 32), 32)],
            gorecv.at[chip],
            o_ssem.at[to],
            o_rsem.at[chip],
            {"dp": 2 * to + core},
        ).start()

    loop(1, 8, send_out)

    thr[...] = jnp.zeros_like(thr)

    def conv_step(a):
        thr[...] += dot(
            amat[pl.ds(pl.multiple_of(64 * a, 64), CELLS), :],
            wconv[pl.ds(pl.multiple_of(3 * W * a, W), 3 * W), :],
        )

    loop(0, 3, conv_step)
    out_ref[...] = thr[...].astype(BF16)
    out_out = pltpu.make_async_copy(out_ref, out_hbm, lsem.at[8])
    out_out.start()

    def take_grad(k):
        frm = lax.rem(chip + k, 8)
        rcopy(grecv.at[frm], grecv.at[frm], g_ssem.at[frm], g_rsem.at[frm], mate).wait_recv()

    loop(1, 8, take_grad)
    grecv[chip] = gst[pl.ds(pl.multiple_of(576 * chip + 288 * core, 32), 288), :]
    sum2[...] = jnp.sum(grecv[...].astype(F32), axis=0)
    piece32[...] = jnp.zeros_like(piece32)
    for t in range(N):
        for q in range(2):
            piece32[pl.ds(q, 18, stride=2), :] = sum2[18 * t : 18 * t + 18, 128 * q : 128 * q + 128]
        piece[t] = piece32[...].astype(BF16)

    def send_piece(k):
        t = lax.rem(s + k, N)
        rcopy(piece.at[t], precv.at[s], p_ssem.at[k], p_rsem.at[s], {"space": t}).start()

    loop(1, N, send_piece)
    precv[s] = piece[s]

    def take_out(k):
        frm = lax.rem(chip + k, 8)
        rcopy(gorecv.at[frm], gorecv.at[frm], o_ssem.at[frm], o_rsem.at[frm], mate).wait_recv()

    loop(1, 8, take_out)
    gorecv[chip] = gost[pl.ds(pl.multiple_of(64 * chip + 32 * core, 32), 32), :]
    out_sum = jnp.sum(gorecv[...].astype(F32), axis=0)
    for t in range(N):
        opiece[t] = pack(out_sum[2 * t : 2 * t + 1], out_sum[2 * t + 1 : 2 * t + 2])

    def send_opiece(k):
        t = lax.rem(s + k, N)
        rcopy(opiece.at[t], oprecv.at[s], op_ssem.at[k], op_rsem.at[s], {"space": t}).start()

    loop(1, N, send_opiece)
    oprecv[s] = opiece[s]

    for p in range(8):
        forward(p).wait_send()
        if p:
            kv_copy(p).wait_send()
            q_copy(p).wait_send()
            rcopy(ats.at[p], atr.at[0], at_ssem.at[p], at_rsem.at[0], other).wait_send()

    def chips_sent(k):
        to = lax.rem(chip + k, 8)
        rcopy(gorecv.at[to], gorecv.at[to], o_ssem.at[to], o_rsem.at[to], mate).wait_send()
        rcopy(grecv.at[to], grecv.at[to], g_ssem.at[to], g_rsem.at[to], mate).wait_send()

    loop(1, 8, chips_sent)
    for copy in (up_mate, up_other, up_both, hid_other, pair_att, pair_act, pair_gf):
        copy.wait_send()

    @pl.when(s > 0)
    def _():
        up_top.wait_send()

    @pl.when(s < N - 1)
    def _():
        up_bottom.wait_send()

    @pl.when(has_far)
    def _():
        hid_far.wait_send()

    gf_out.wait()
    out_out.wait()

    def take_pieces(k):
        t = lax.rem(s + k, N)
        g = rcopy(piece.at[t], precv.at[t], p_ssem.at[k], p_rsem.at[t], {"space": t})
        g.wait_send()
        g.wait_recv()

    loop(1, N, take_pieces)
    for side in range(2):
        total = precv[side].astype(F32)
        for i in range(1, 8):
            total += precv[2 * i + side].astype(F32)
        piece32[...] = total
        for q in range(2):
            gc_ref[pl.ds(2 * side + q, 18, stride=4), :] = piece32[pl.ds(q, 18, stride=2), :]

    def take_opieces(k):
        t = lax.rem(s + k, N)
        o = rcopy(opiece.at[t], oprecv.at[t], op_ssem.at[k], op_rsem.at[t], {"space": t})
        o.wait_send()
        o.wait_recv()

    loop(1, N, take_opieces)
    go_ref[...] = jnp.sum(oprecv[...], axis=0)


def hand_on(*refs):
    ins, outs, kept, sem = refs[:4], refs[4:8], refs[8:12], refs[12]
    first = [pltpu.make_async_copy(a, b, sem.at[0, i]) for i, (a, b) in enumerate(zip(ins, kept))]
    then = [pltpu.make_async_copy(a, b, sem.at[1, i]) for i, (a, b) in enumerate(zip(kept, outs))]
    for copy in first:
        copy.start()
    for came, goes in zip(first, then):
        came.wait()
        goes.start()
    for copy in then:
        copy.wait()


def time_features(timestep):
    halfway = TFEAT // 2
    frequency = jnp.exp(-math.log(10000.0) * jnp.arange(halfway, dtype=F32) / halfway)
    angles = timestep.astype(F32)[:, None] * frequency[None, :]
    return jnp.concatenate([jnp.cos(angles), jnp.sin(angles)], axis=1)


def on_device(features, timestep, w_time, w_emb, w_qkv, w_out, w_conv, upstream):
    tfeat = jnp.broadcast_to(time_features(timestep), (8, TFEAT))
    vmem = pl.BlockSpec(memory_space=pltpu.VMEM)
    hbm = pl.BlockSpec(memory_space=pl.ANY)
    V = pltpu.VMEM
    dma = pltpu.SemaphoreType.DMA
    scratch = [
        V((CELLS, W), BF16), V((TFEAT, W), BF16), V((W, 2 * W), BF16), V((W, 3 * W), BF16),
        V((W, W), BF16), V((9 * W, W), BF16),
        V((N, 8, 128), F32), V((N, 8, 128), F32), V((N, 8, 128), F32),
        V((8, CELLS, 128), BF16), V((8, 128, 128), BF16), V((N, CELLS, 128), BF16), V((8, 128, 128), BF16),
        V((8, CELLS, 128), BF16), V((N, CELLS, 128), BF16), V((8, CELLS, 128), F32), V((8, CELLS, 128), F32),
        V((8, 128, 128), BF16), V((8, 128, 128), BF16), V((CELLS, W), BF16),
        V((384, W), BF16), V((384, HALF), BF16), V((4, 384, HALF), BF16), V((384, 3 * W), BF16),
        V((4, 384, 3 * HALF), BF16),
        V((CELLS, W), BF16), V((CELLS, W), BF16), V((64, W), BF16), V((384, W), BF16), V((CELLS, W), BF16),
        V((384, 3 * W), BF16), V((CELLS, W), BF16), V((CELLS, W), BF16), V((CELLS, W), BF16),
        V((W, 4 * CELLS), BF16), V((W, 2 * CELLS), BF16),
        V((CELLS, W), BF16), V((CELLS, W), F32), V((CELLS, W), F32), V((CELLS, W), F32), V((CELLS, W), F32),
        V((8, 2 * W), F32),
        V((9 * W, HALF), BF16), V((8, 288, HALF), BF16), V((W, W), BF16), V((8, 32, W), BF16),
        V((288, HALF), F32), V((48, 128), F32), V((N, 48, 128), BF16), V((N, 48, 128), BF16),
        V((N, 8, 128), F32), V((N, 8, 128), F32),
        dma((9,)),
        dma((3, N)), dma((3, N)),
        dma((8,)), dma((N,)), dma((8,)), dma((8,)), dma((8,)), dma((8,)), dma((8,)),
        dma((3,)), dma((3,)), dma((7,)), dma((7,)),
        dma((8,)), dma((8,)), dma((8,)), dma((8,)), dma((N,)), dma((N,)), dma((N,)), dma((N,)),
    ]
    shapes = (
        jax.ShapeDtypeStruct((CELLS, W), BF16),
        jax.ShapeDtypeStruct((CELLS, W), BF16),
        jax.ShapeDtypeStruct((72, 128), F32),
        jax.ShapeDtypeStruct((8, 128), F32),
    )
    made = pl.pallas_call(
        kernel,
        out_shape=shapes,
        in_specs=[hbm, vmem, hbm, hbm, hbm, hbm, hbm, hbm],
        out_specs=(hbm, hbm, vmem, vmem),
        scratch_shapes=scratch,
        compiler_params=pltpu.CompilerParams(
            collective_id=0, has_side_effects=True, vmem_limit_bytes=60 * 1024 * 1024
        ),
    )(
        features.reshape(CELLS, W), tfeat, upstream.reshape(CELLS, W),
        w_time, w_emb, w_qkv, w_out, w_conv,
    )
    out, gf, gc, go = pl.pallas_call(
        hand_on,
        out_shape=shapes,
        in_specs=[hbm] * 4,
        out_specs=(hbm,) * 4,
        scratch_shapes=[V(shape.shape, shape.dtype) for shape in shapes] + [dma((2, 4))],
    )(*made)
    return (
        out.reshape(features.shape),
        gf.reshape(features.shape),
        gc.reshape(-1),
        go.reshape(-1),
    )


def solution(mesh):
    return jax.shard_map(
        on_device,
        mesh=mesh,
        in_specs=(
            P("dp", "space", None, None), P("dp"), P(), P(), P(), P(), P(),
            P("dp", "space", None, None),
        ),
        out_specs=(
            P("dp", "space", None, None), P("dp", "space", None, None),
            P(("dp", "space")), P(("dp", "space")),
        ),
        check_vma=False,
    )
```

time: 130 us -> 102 us (0.78)
  the two profiles are of different devices: /device:TPU:1 before, /device:TPU:14 now
where the time goes in v2:
time: 102 us
  Pallas kernels  99.5 us (98%)
  between operations  1.29 us (1%)
    pallas_call x1, Pallas kernels, on_device(): pl.pallas_call(kernel, out_shape=shapes, in_specs=[hbm, vmem, hbm, hbm, h...  97.7 us

profile of v2, /device:TPU:14, one launch (start us, length us, event | category | flops | bytes accessed | tf_op | source)
XLA Modules:
  0.0 101.5 jit_solution(152214938579043134)
XLA Ops:
  1.3 0.1 fusion
  1.3 0.1 maximum_bitcast_fusion
  1.4 0.6 broadcast_in_dim.10.tf_ref
  2.0 97.7 %shard_map.111 = (bf16[256,512]{1,0:T(8,128)(2,1)}, bf16[256,512]{1,0:T(8,128)(2,1)}, f32[72,128]{1,0:T(8,128)}, f32[8,128]{1,0:T(8,128)}) custom-call(bf16[256,512]{1,0:T(8,128)(2,1)} %bitcast.9, f32[8,128]{1,0:T(8,128)} %broadcast_in_dim.10.tf_ref, bf16[256,512]{1,0:T(8,128)(2,1)} %bitcast.10, bf16[128,512]{1,0:T(8,128)(2,1)} %wtime_hbm.1, ...), custom_call_target="tpu_custom_call" | custom-call | tf_op jit(solution)/shard_map/pallas_call | solution.py:668
  99.7 1.8 %shard_map.112 = (bf16[256,512]{1,0:T(8,128)(2,1)}, bf16[256,512]{1,0:T(8,128)(2,1)}, f32[72,128]{1,0:T(8,128)}, f32[8,128]{1,0:T(8,128)}) custom-call(bf16[256,512]{1,0:T(8,128)(2,1)} %get-tuple-element.12.refs_0_, bf16[256,512]{1,0:T(8,128)(2,1)} %get-tuple-element.13.refs_1_, f32[72,128]{1,0:T(8,128)} %get-tuple-element.14.refs_2_, ...), custom_call_target="tpu_custom_call" | custom-call | tf_op jit(solution)/shard_map/pallas_call | solution.py:681

commit v3 on v2

--- a/solution.py
+++ b/solution.py
@@ -35,8 +35,13 @@
     lax.fori_loop(lo, hi, body, 0)
 
 
+def far_first(i):
+    return 8 + jnp.where(lax.rem(i, 2) == 1, i // 2, -(i // 2))
+
+
 def share_start(buf, ssem, rsem, s):
-    def go(k):
+    def go(i):
+        k = far_first(i)
         t = lax.rem(s + k, N)
         rcopy(buf.at[s], buf.at[s], ssem.at[k], rsem.at[s], {"space": t}).start()
 
@@ -123,7 +128,7 @@
     out_hbm, gf_hbm, gc_ref, go_ref,
     x_ref, wtime, wemb, wqkv, wout, wconv,
     st1, st2, st3,
-    kvs, qs, kvr, qr, qq, val, top, acc, ats, atr, att,
+    kvs, qs, kvr, qr, qq, val, top, acc, score, ats, atr, att,
     upp, uo, uh, umat, umat4,
     hid, hx, hfar, actp, xact, amat, patt, gf_ref, pgf, actt, attt,
     out_ref, hat, zed, back, thr, mod,
@@ -143,15 +148,6 @@
     mate = {"dp": 2 * chip + 1 - core}
     other = {"space": 2 * z + 1 - xl}
 
-    barrier = pltpu.get_barrier_semaphore()
-
-    def greet(dev):
-        pl.semaphore_signal(barrier, inc=1, device_id=dev, device_id_type=MESH)
-
-    loop(1, N, lambda k: greet({"space": lax.rem(s + k, N)}))
-    loop(1, 8, lambda k: greet({"dp": 2 * lax.rem(chip + k, 8) + core}))
-    greet(mate)
-
     loads = [
         pltpu.make_async_copy(a, b, lsem.at[i])
         for i, (a, b) in enumerate(
@@ -169,6 +165,15 @@
     loads[0].start()
     loads[1].start()
 
+    barrier = pltpu.get_barrier_semaphore()
+
+    def greet(dev):
+        pl.semaphore_signal(barrier, inc=1, device_id=dev, device_id_type=MESH)
+
+    loop(1, N, lambda i: greet({"space": lax.rem(s + far_first(i), N)}))
+    loop(1, 8, lambda k: greet({"dp": 2 * lax.rem(chip + k, 8) + core}))
+    greet(mate)
+
     blank = jnp.zeros((64, W), BF16)
 
     @pl.when(s == 0)
@@ -250,7 +255,7 @@
 
     loads[3].wait()
     loads[4].wait()
-    embedded = exact_dot(tf_ref[...], wtime[...])
+    embedded = exact_dot(jnp.broadcast_to(tf_ref[...], (8, TFEAT)), wtime[...])
     mod[...] = exact_dot(silu(embedded), wemb[...])
 
     @pl.when(s < N - 1)
@@ -267,12 +272,13 @@
     up_other = rcopy(uo, uh.at[1], pair_ssem.at[1], pair_rsem.at[1], other)
     up_both = rcopy(uh.at[1], uh.at[3], pair_ssem.at[2], pair_rsem.at[2], mate)
     up_mate.start()
-    up_other.start()
     windows(upp[...].astype(F32), umat)
     windows(uh[0].astype(F32), umat4.at[0])
     loads[5].wait()
     loads[6].wait()
     back[...] = jnp.zeros_like(back)
+    kv_copy(3).start()
+    kv_copy(4).start()
 
     def back_step(p):
         a = p // 3
@@ -285,8 +291,8 @@
 
     for p in range(1, 8):
         q_copy(NEAR.index((8 - NEAR[p]) % 8)).wait_recv()
-    kv_copy(3).start()
-    kv_copy(4).start()
+    kv_copy(5).start()
+    kv_copy(6).start()
     for p in range(8):
         q = qr[p].astype(F32)
         qq[p, 0:128, :] = jnp.where(low_short, q, 0.0).astype(BF16)
@@ -300,12 +306,14 @@
             forward(p - 8).wait_recv()
         val[p] = jnp.where(low_half, 1.0, kvr[p].astype(F32)).astype(BF16)
 
-    def attend(i, slots, first, last):
-        query = qq[i]
-        parts = [dot_nt(query, kvr[p]) for p in slots]
+    def scores(i, slots, b):
+        for j, p in enumerate(slots):
+            score[b, j] = dot_nt(qq[i], kvr[p])
+
+    def attend(i, slots, b, first, last):
         high = None
-        for part in parts:
-            part = jnp.maximum(part[:, 0:128], part[:, 128:256])
+        for j in range(len(slots)):
+            part = jnp.maximum(score[b, j, :, 0:128], score[b, j, :, 128:256])
             high = part if high is None else jnp.maximum(high, part)
         high = jnp.max(high, axis=1, keepdims=True) * LOG2E
         if not first:
@@ -315,60 +323,71 @@
             high = jnp.broadcast_to(high, (CELLS, 128))
         wide = jnp.concatenate([high, high], axis=1)
         total = None
-        for part, p in zip(parts, slots):
-            mixed = dot(jnp.exp2(part * LOG2E - wide).astype(BF16), val[p])
+        for j, p in enumerate(slots):
+            mixed = dot(jnp.exp2(score[b, j] * LOG2E - wide).astype(BF16), val[p])
             total = mixed if total is None else total + mixed
         if not first:
             total = total + acc[i] * jnp.exp2(before - high)
-        if last:
-            return total
-        top[i] = high
-        acc[i] = total
+        if not last:
+            top[i] = high
+            acc[i] = total
+        return total
 
     def finish(total):
         ratio = total / pltpu.roll(total, 64, 1)
         return jnp.where(low_short, pltpu.roll(ratio[0:128], 64, 1), ratio[128:256]).astype(BF16)
 
     def go(*slots):
-        loop(0, 8, lambda i: attend(i, slots, 0 in slots, False))
+        first, last = 0 in slots, 15 in slots
+
+        def use(i, b):
+            total = attend(i, slots, b, first, last)
+            if last:
+                ats[i] = finish(total)
+
+                @pl.when(i > 0)
+                def _():
+                    away = jnp.where(lax.rem(i, 2) == 1, (i + 1) // 2, 8 - i // 2)
+                    there = 2 * lax.rem(z + away, 8) + xl
+                    rcopy(
+                        ats.at[i], atr.at[z], at_ssem.at[i], at_rsem.at[z], {"space": there}
+                    ).start()
+
+        def turn(k):
+            return 7 - k if last else k
+
+        def step(m):
+            k = 2 * m
+            scores(turn(k + 1), slots, 1)
+            use(turn(k), 0)
+            scores(turn(jnp.minimum(k + 2, 7)), slots, 0)
+            use(turn(k + 1), 1)
+
+        scores(turn(0), slots, 0)
+        loop(0, 4, step)
 
     take(0)
+    take(8)
     take(1)
     take(2)
-    kv_copy(5).start()
-    kv_copy(6).start()
-    go(0, 1, 2)
+    kv_copy(7).start()
+    go(0, 8, 1, 2)
     take(3)
     take(4)
-    kv_copy(7).start()
-    up_other.wait_recv()
-    up_both.start()
-    take(8)
-    go(3, 4, 8)
     take(9)
     take(10)
+    go(3, 4, 9, 10)
     take(5)
     take(6)
-    go(9, 10, 5, 6)
-    take(7)
     take(11)
     take(12)
-    go(7, 11, 12)
-    for p in (13, 14, 15):
+    go(5, 6, 11, 12)
+    for p in (7, 13, 14, 15):
         take(p)
-
-    def last_far(k):
-        i = 8 - k
-        zz = lax.rem(z + jnp.where(lax.rem(i, 2) == 1, (i + 1) // 2, 8 - i // 2), 8)
-        ats[i] = finish(attend(i, (13, 14, 15), False, True))
-        rcopy(
-            ats.at[i], atr.at[z], at_ssem.at[i], at_rsem.at[z], {"space": 2 * zz + xl}
-        ).start()
-
-    loop(1, 8, last_far)
-    atr[z] = finish(attend(0, (13, 14, 15), False, True))
-
-    windows(uh[1].astype(F32), umat4.at[1])
+    up_other.start()
+    go(7, 13, 14, 15)
+    atr[z] = ats[0]
+
     for k in range(1, 8):
         h = lax.rem(z + k, 8)
         rcopy(ats.at[k], atr.at[h], at_ssem.at[k], at_rsem.at[h], other).wait_recv()
@@ -399,6 +418,9 @@
     hid_other.start()
     pair_att = rcopy(att, patt, pair_ssem.at[4], pair_rsem.at[4], mate)
     pair_att.start()
+    up_other.wait_recv()
+    up_both.start()
+    windows(uh[1].astype(F32), umat4.at[1])
     up_mate.wait_recv()
     windows(uh[2].astype(F32), umat4.at[2])
     up_both.wait_recv()
@@ -457,6 +479,15 @@
     windows(actp[...].astype(F32), amat)
     pair_act.wait_recv()
 
+    def grad_copy(half, to):
+        return rcopy(
+            gst.at[pl.ds(pl.multiple_of(576 * to + 288 * core + 144 * half, 16), 144)],
+            grecv.at[chip, pl.ds(144 * half, 144)],
+            g_ssem.at[half, to],
+            g_rsem.at[half, chip],
+            {"dp": 2 * to + core},
+        )
+
     def grad_step(j):
         p = lax.rem(chip + 1 + j, 9)
         a = p // 3
@@ -470,14 +501,7 @@
 
         @pl.when((j >= 1) & (p >= 1))
         def _():
-            to = p - 1
-            rcopy(
-                gst.at[pl.ds(pl.multiple_of(576 * to + 288 * core, 32), 288)],
-                grecv.at[chip],
-                g_ssem.at[to],
-                g_rsem.at[chip],
-                {"dp": 2 * to + core},
-            ).start()
+            grad_copy(0, p - 1).start()
 
     loop(0, 9, grad_step)
 
@@ -503,6 +527,7 @@
         ).start()
 
     loop(1, 8, send_out)
+    loop(1, 8, lambda k: grad_copy(1, lax.rem(chip + k, 8)).start())
 
     thr[...] = jnp.zeros_like(thr)
 
@@ -517,25 +542,40 @@
     out_out = pltpu.make_async_copy(out_ref, out_hbm, lsem.at[8])
     out_out.start()
 
-    def take_grad(k):
-        frm = lax.rem(chip + k, 8)
-        rcopy(grecv.at[frm], grecv.at[frm], g_ssem.at[frm], g_rsem.at[frm], mate).wait_recv()
-
-    loop(1, 8, take_grad)
-    grecv[chip] = gst[pl.ds(pl.multiple_of(576 * chip + 288 * core, 32), 288), :]
-    sum2[...] = jnp.sum(grecv[...].astype(F32), axis=0)
+    def second(half):
+        def take_grad(k):
+            frm = lax.rem(chip + k, 8)
+            part = grecv.at[frm, pl.ds(144 * half, 144)]
+            rcopy(part, part, g_ssem.at[half, frm], g_rsem.at[half, frm], mate).wait_recv()
+
+        loop(1, 8, take_grad)
+        grecv[chip, 144 * half : 144 * half + 144] = gst[
+            pl.ds(pl.multiple_of(576 * chip + 288 * core + 144 * half, 16), 144), :
+        ]
+        sum2[...] = jnp.sum(grecv[:, 144 * half : 144 * half + 144].astype(F32), axis=0)
+        for i in range(8):
+            t = 8 * half + i
+            for q in range(2):
+                piece32[pl.ds(q, 18, stride=2), :] = sum2[
+                    18 * i : 18 * i + 18, 128 * q : 128 * q + 128
+                ]
+            piece[t] = piece32[...].astype(BF16)
+
+        def send_piece(i):
+            t = 8 * half + i
+
+            @pl.when(t != s)
+            def _():
+                rcopy(piece.at[t], precv.at[s], p_ssem.at[t], p_rsem.at[s], {"space": t}).start()
+
+            @pl.when(t == s)
+            def _():
+                precv[s] = piece[s]
+
+        loop(0, 8, send_piece)
+
     piece32[...] = jnp.zeros_like(piece32)
-    for t in range(N):
-        for q in range(2):
-            piece32[pl.ds(q, 18, stride=2), :] = sum2[18 * t : 18 * t + 18, 128 * q : 128 * q + 128]
-        piece[t] = piece32[...].astype(BF16)
-
-    def send_piece(k):
-        t = lax.rem(s + k, N)
-        rcopy(piece.at[t], precv.at[s], p_ssem.at[k], p_rsem.at[s], {"space": t}).start()
-
-    loop(1, N, send_piece)
-    precv[s] = piece[s]
+    second(0)
 
     def take_out(k):
         frm = lax.rem(chip + k, 8)
@@ -553,6 +593,7 @@
 
     loop(1, N, send_opiece)
     oprecv[s] = opiece[s]
+    second(1)
 
     for p in range(8):
         forward(p).wait_send()
@@ -564,7 +605,8 @@
     def chips_sent(k):
         to = lax.rem(chip + k, 8)
         rcopy(gorecv.at[to], gorecv.at[to], o_ssem.at[to], o_rsem.at[to], mate).wait_send()
-        rcopy(grecv.at[to], grecv.at[to], g_ssem.at[to], g_rsem.at[to], mate).wait_send()
+        grad_copy(0, to).wait_send()
+        grad_copy(1, to).wait_send()
 
     loop(1, 8, chips_sent)
     for copy in (up_mate, up_other, up_both, hid_other, pair_att, pair_act, pair_gf):
@@ -587,7 +629,7 @@
 
     def take_pieces(k):
         t = lax.rem(s + k, N)
-        g = rcopy(piece.at[t], precv.at[t], p_ssem.at[k], p_rsem.at[t], {"space": t})
+        g = rcopy(piece.at[t], precv.at[t], p_ssem.at[t], p_rsem.at[t], {"space": t})
         g.wait_send()
         g.wait_recv()
 
@@ -631,7 +673,7 @@
 
 
 def on_device(features, timestep, w_time, w_emb, w_qkv, w_out, w_conv, upstream):
-    tfeat = jnp.broadcast_to(time_features(timestep), (8, TFEAT))
+    tfeat = time_features(timestep)
     vmem = pl.BlockSpec(memory_space=pltpu.VMEM)
     hbm = pl.BlockSpec(memory_space=pl.ANY)
     V = pltpu.VMEM
@@ -642,7 +684,7 @@
         V((N, 8, 128), F32), V((N, 8, 128), F32), V((N, 8, 128), F32),
         V((8, CELLS, 128), BF16), V((8, 128, 128), BF16), V((N, CELLS, 128), BF16), V((8, 128, 128), BF16),
         V((8, CELLS, 128), BF16), V((N, CELLS, 128), BF16), V((8, CELLS, 128), F32), V((8, CELLS, 128), F32),
-        V((8, 128, 128), BF16), V((8, 128, 128), BF16), V((CELLS, W), BF16),
+        V((2, 4, CELLS, CELLS), F32), V((8, 128, 128), BF16), V((8, 128, 128), BF16), V((CELLS, W), BF16),
         V((384, W), BF16), V((384, HALF), BF16), V((4, 384, HALF), BF16), V((384, 3 * W), BF16),
         V((4, 384, 3 * HALF), BF16),
         V((CELLS, W), BF16), V((CELLS, W), BF16), V((64, W), BF16), V((384, W), BF16), V((CELLS, W), BF16),
@@ -651,13 +693,13 @@
         V((CELLS, W), BF16), V((CELLS, W), F32), V((CELLS, W), F32), V((CELLS, W), F32), V((CELLS, W), F32),
         V((8, 2 * W), F32),
         V((9 * W, HALF), BF16), V((8, 288, HALF), BF16), V((W, W), BF16), V((8, 32, W), BF16),
-        V((288, HALF), F32), V((48, 128), F32), V((N, 48, 128), BF16), V((N, 48, 128), BF16),
+        V((144, HALF), F32), V((48, 128), F32), V((N, 48, 128), BF16), V((N, 48, 128), BF16),
         V((N, 8, 128), F32), V((N, 8, 128), F32),
         dma((9,)),
         dma((3, N)), dma((3, N)),
         dma((8,)), dma((N,)), dma((8,)), dma((8,)), dma((8,)), dma((8,)), dma((8,)),
         dma((3,)), dma((3,)), dma((7,)), dma((7,)),
-        dma((8,)), dma((8,)), dma((8,)), dma((8,)), dma((N,)), dma((N,)), dma((N,)), dma((N,)),
+        dma((2, 8)), dma((2, 8)), dma((8,)), dma((8,)), dma((N,)), dma((N,)), dma((N,)), dma((N,)),
     ]
     shapes = (
         jax.ShapeDtypeStruct((CELLS, W), BF16),

time: 102 us -> 93.3 us (0.915)
  the two profiles are of different devices: /device:TPU:14 before, /device:TPU:1 now
where the time goes in v3:
time: 93.3 us; the launch traced here: 93 us
  Pallas kernels  91.1 us (98%)
  between operations  1.29 us (1%)
    pallas_call x1, Pallas kernels, on_device(): pl.pallas_call(kernel, out_shape=shapes, in_specs=[hbm, vmem, hbm, hbm, h...  89.3 us

profile of v3, /device:TPU:1, one launch (start us, length us, event | category | flops | bytes accessed | tf_op | source)
XLA Modules:
  0.0 93.0 jit_solution(15048036368864751796)
XLA Ops:
  1.3 0.1 fusion
  1.3 0.6 pad_maximum_fusion.tf_ref
  1.9 89.3 %shard_map.111 = (bf16[256,512]{1,0:T(8,128)(2,1)}, bf16[256,512]{1,0:T(8,128)(2,1)}, f32[72,128]{1,0:T(8,128)}, f32[8,128]{1,0:T(8,128)}) custom-call(bf16[256,512]{1,0:T(8,128)(2,1)} %bitcast.7, f32[1,128]{1,0:T(1,128)} %pad_maximum_fusion.tf_ref, bf16[256,512]{1,0:T(8,128)(2,1)} %bitcast.8, bf16[128,512]{1,0:T(8,128)(2,1)} %wtime_hbm.1, ...), custom_call_target="tpu_custom_call" | custom-call | tf_op jit(solution)/shard_map/pallas_call | solution.py:710
  91.2 1.8 %shard_map.112 = (bf16[256,512]{1,0:T(8,128)(2,1)}, bf16[256,512]{1,0:T(8,128)(2,1)}, f32[72,128]{1,0:T(8,128)}, f32[8,128]{1,0:T(8,128)}) custom-call(bf16[256,512]{1,0:T(8,128)(2,1)} %get-tuple-element.12.refs_0_, bf16[256,512]{1,0:T(8,128)(2,1)} %get-tuple-element.13.refs_1_, f32[72,128]{1,0:T(8,128)} %get-tuple-element.14.refs_2_, ...), custom_call_target="tpu_custom_call" | custom-call | tf_op jit(solution)/shard_map/pallas_call | solution.py:723

commit v4 on v3

--- a/solution.py
+++ b/solution.py
@@ -124,7 +124,7 @@
 
 
 def kernel(
-    x_hbm, tf_ref, up_hbm, wtime_hbm, wemb_hbm, wqkv_hbm, wout_hbm, wconv_hbm,
+    x_hbm, t_ref, up_hbm, wtime_hbm, wemb_hbm, wqkv_hbm, wout_hbm, wconv_hbm,
     out_hbm, gf_hbm, gc_ref, go_ref,
     x_ref, wtime, wemb, wqkv, wout, wconv,
     st1, st2, st3,
@@ -133,11 +133,12 @@
     hid, hx, hfar, actp, xact, amat, patt, gf_ref, pgf, actt, attt,
     out_ref, hat, zed, back, thr, mod,
     gst, grecv, gost, gorecv, sum2, piece32, piece, precv, opiece, oprecv,
+    wide32, pack32, zpiece, zrecv, fpiece, frecv,
     lsem,
     st_ssem, st_rsem,
     kv_ssem, kv_rsem, fw_ssem, q_ssem, q_rsem, at_ssem, at_rsem,
     halo_ssem, halo_rsem, pair_ssem, pair_rsem,
-    g_ssem, g_rsem, o_ssem, o_rsem, p_ssem, p_rsem, op_ssem, op_rsem,
+    g_ssem, g_rsem, o_ssem, o_rsem, p_ssem, p_rsem, op_ssem, op_rsem, z_ssem, z_rsem, f_ssem, f_rsem,
 ):
     d = lax.axis_index("dp")
     s = lax.axis_index("space")
@@ -147,6 +148,7 @@
     core = lax.rem(d, 2)
     mate = {"dp": 2 * chip + 1 - core}
     other = {"space": 2 * z + 1 - xl}
+    afar = 2 * lax.rem(chip // 2 + 2, 4) + 1 - lax.rem(chip, 2)
 
     loads = [
         pltpu.make_async_copy(a, b, lsem.at[i])
@@ -173,6 +175,7 @@
     loop(1, N, lambda i: greet({"space": lax.rem(s + far_first(i), N)}))
     loop(1, 8, lambda k: greet({"dp": 2 * lax.rem(chip + k, 8) + core}))
     greet(mate)
+    greet({"dp": 2 * afar + core, "space": 2 * z + 1 - xl})
 
     blank = jnp.zeros((64, W), BF16)
 
@@ -188,7 +191,7 @@
     st1[s] = local_moments(x_ref[...].astype(F32))
     for load in loads[2:]:
         load.start()
-    pl.semaphore_wait(barrier, 15 + 7 + 1)
+    pl.semaphore_wait(barrier, 15 + 7 + 1 + 1)
     share_start(st1, st_ssem.at[0], st_rsem.at[0], s)
 
     loads[2].wait()
@@ -255,7 +258,10 @@
 
     loads[3].wait()
     loads[4].wait()
-    embedded = exact_dot(jnp.broadcast_to(tf_ref[...], (8, TFEAT)), wtime[...])
+    spot = lax.broadcasted_iota(jnp.int32, (8, TFEAT), 1)
+    nth = (spot & (TFEAT // 2 - 1)).astype(F32)
+    angle = t_ref[0].astype(F32) * jnp.exp(-math.log(10000.0) * nth / (TFEAT // 2))
+    embedded = exact_dot(jnp.where(spot < TFEAT // 2, jnp.cos(angle), jnp.sin(angle)), wtime[...])
     mod[...] = exact_dot(silu(embedded), wemb[...])
 
     @pl.when(s < N - 1)
@@ -444,15 +450,14 @@
     sigma = jax.nn.sigmoid(shifted)
     act = (shifted * sigma).astype(BF16)
     actp[64:320, :] = act
-    actt[:, 0:CELLS] = act.T
+    actt[0] = act.T
+    pair_act = rcopy(actt.at[0], actt.at[2], pair_ssem.at[5], pair_rsem.at[5], mate)
+    pair_act.start()
     hid_other.wait_recv()
     xact[...] = act_of(hx)
-    actt[:, CELLS : 2 * CELLS] = xact[...].T
-    pair_act = rcopy(
-        actt.at[:, pl.ds(0, 2 * CELLS)], actt.at[:, pl.ds(2 * CELLS, 2 * CELLS)],
-        pair_ssem.at[5], pair_rsem.at[5], mate,
-    )
-    pair_act.start()
+    actt[1] = xact[...].T
+    pair_xact = rcopy(actt.at[1], actt.at[3], pair_ssem.at[7], pair_rsem.at[7], mate)
+    pair_xact.start()
 
     through = back[...] * sigma * (1.0 + shifted * (1.0 - sigma)) * scale
     thr[...] = through
@@ -478,6 +483,7 @@
 
     windows(actp[...].astype(F32), amat)
     pair_act.wait_recv()
+    pair_xact.wait_recv()
 
     def grad_copy(half, to):
         return rcopy(
@@ -494,12 +500,12 @@
         b = lax.rem(p, 3)
         rows = pl.ds(pl.multiple_of(64 * (2 - a), 64), CELLS)
         lanes = pl.ds(pl.multiple_of(HALF * (2 - b), HALF), HALF)
-        part = dot(actt[:, 0:CELLS], umat4[0, rows, lanes])
+        part = dot(actt[0], umat4[0, rows, lanes])
         for i in range(1, 4):
-            part += dot(actt[:, CELLS * i : CELLS * i + CELLS], umat4[i, rows, lanes])
+            part += dot(actt[i], umat4[i, rows, lanes])
         gst[pl.ds(pl.multiple_of(W * p, W), W), :] = part.astype(BF16)
 
-        @pl.when((j >= 1) & (p >= 1))
+        @pl.when((j >= 1) & (p >= 1) & (p - 1 != afar))
         def _():
             grad_copy(0, p - 1).start()
 
@@ -527,7 +533,34 @@
         ).start()
 
     loop(1, 8, send_out)
-    loop(1, 8, lambda k: grad_copy(1, lax.rem(chip + k, 8)).start())
+
+    def near_chips(fn):
+        def go(k):
+            to = lax.rem(chip + k, 8)
+
+            @pl.when(to != afar)
+            def _():
+                fn(to)
+
+        loop(1, 8, go)
+
+    near_chips(lambda to: grad_copy(1, to).start())
+    rows_afar = gst[pl.ds(pl.multiple_of(576 * afar + 288 * core, 32), 288), :]
+    wide32[...] = rows_afar.astype(F32)
+    pack32[...] = jnp.zeros_like(pack32)
+    for i in range(8):
+        for q in range(2):
+            pack32[pl.ds(q, 36, stride=2), :] = wide32[36 * i : 36 * i + 36, 128 * q : 128 * q + 128]
+        zpiece[i] = pack32[...].astype(BF16)
+
+    def z_copy(k):
+        h = lax.rem(z + k, 8)
+        return rcopy(
+            zpiece.at[h], zrecv.at[z], z_ssem.at[h], z_rsem.at[z], {"space": 2 * h + xl}
+        )
+
+    loop(1, 8, lambda k: z_copy(k).start())
+    zrecv[z] = zpiece[z]
 
     thr[...] = jnp.zeros_like(thr)
 
@@ -543,12 +576,11 @@
     out_out.start()
 
     def second(half):
-        def take_grad(k):
-            frm = lax.rem(chip + k, 8)
+        def take_grad(frm):
             part = grecv.at[frm, pl.ds(144 * half, 144)]
             rcopy(part, part, g_ssem.at[half, frm], g_rsem.at[half, frm], mate).wait_recv()
 
-        loop(1, 8, take_grad)
+        near_chips(take_grad)
         grecv[chip, 144 * half : 144 * half + 144] = gst[
             pl.ds(pl.multiple_of(576 * chip + 288 * core + 144 * half, 16), 144), :
         ]
@@ -575,7 +607,26 @@
         loop(0, 8, send_piece)
 
     piece32[...] = jnp.zeros_like(piece32)
+    grecv[afar] = jnp.zeros((288, HALF), BF16)
     second(0)
+
+    def take_z(k):
+        h = lax.rem(z + k, 8)
+        rcopy(zpiece.at[h], zrecv.at[h], z_ssem.at[h], z_rsem.at[h], other).wait_recv()
+
+    loop(1, 8, take_z)
+    pack32[...] = jnp.sum(zrecv[...].astype(F32), axis=0)
+
+    def far_copy(side):
+        return rcopy(
+            fpiece.at[side], frecv.at[xl], f_ssem.at[side], f_rsem.at[xl],
+            {"dp": 2 * afar + core, "space": 2 * z + side},
+        )
+
+    for side in range(2):
+        piece32[0:36, :] = pack32[36 * side : 36 * side + 36, :]
+        fpiece[side] = piece32[...].astype(BF16)
+        far_copy(side).start()
 
     def take_out(k):
         frm = lax.rem(chip + k, 8)
@@ -605,11 +656,17 @@
     def chips_sent(k):
         to = lax.rem(chip + k, 8)
         rcopy(gorecv.at[to], gorecv.at[to], o_ssem.at[to], o_rsem.at[to], mate).wait_send()
-        grad_copy(0, to).wait_send()
-        grad_copy(1, to).wait_send()
+        z_copy(k).wait_send()
+
+        @pl.when(to != afar)
+        def _():
+            grad_copy(0, to).wait_send()
+            grad_copy(1, to).wait_send()
 
     loop(1, 8, chips_sent)
-    for copy in (up_mate, up_other, up_both, hid_other, pair_att, pair_act, pair_gf):
+    far_copy(0).wait_send()
+    far_copy(1).wait_send()
+    for copy in (up_mate, up_other, up_both, hid_other, pair_att, pair_act, pair_xact, pair_gf):
         copy.wait_send()
 
     @pl.when(s > 0)
@@ -635,7 +692,10 @@
 
     loop(1, N, take_pieces)
     for side in range(2):
-        total = precv[side].astype(F32)
+        rcopy(
+            fpiece.at[side], frecv.at[side], f_ssem.at[side], f_rsem.at[side], other
+        ).wait_recv()
+        total = precv[side].astype(F32) + frecv[side].astype(F32)
         for i in range(1, 8):
             total += precv[2 * i + side].astype(F32)
         piece32[...] = total
@@ -665,15 +725,7 @@
         copy.wait()
 
 
-def time_features(timestep):
-    halfway = TFEAT // 2
-    frequency = jnp.exp(-math.log(10000.0) * jnp.arange(halfway, dtype=F32) / halfway)
-    angles = timestep.astype(F32)[:, None] * frequency[None, :]
-    return jnp.concatenate([jnp.cos(angles), jnp.sin(angles)], axis=1)
-
-
 def on_device(features, timestep, w_time, w_emb, w_qkv, w_out, w_conv, upstream):
-    tfeat = time_features(timestep)
     vmem = pl.BlockSpec(memory_space=pltpu.VMEM)
     hbm = pl.BlockSpec(memory_space=pl.ANY)
     V = pltpu.VMEM
@@ -689,17 +741,20 @@
         V((4, 384, 3 * HALF), BF16),
         V((CELLS, W), BF16), V((CELLS, W), BF16), V((64, W), BF16), V((384, W), BF16), V((CELLS, W), BF16),
         V((384, 3 * W), BF16), V((CELLS, W), BF16), V((CELLS, W), BF16), V((CELLS, W), BF16),
-        V((W, 4 * CELLS), BF16), V((W, 2 * CELLS), BF16),
+        V((4, W, CELLS), BF16), V((W, 2 * CELLS), BF16),
         V((CELLS, W), BF16), V((CELLS, W), F32), V((CELLS, W), F32), V((CELLS, W), F32), V((CELLS, W), F32),
         V((8, 2 * W), F32),
         V((9 * W, HALF), BF16), V((8, 288, HALF), BF16), V((W, W), BF16), V((8, 32, W), BF16),
         V((144, HALF), F32), V((48, 128), F32), V((N, 48, 128), BF16), V((N, 48, 128), BF16),
         V((N, 8, 128), F32), V((N, 8, 128), F32),
+        V((288, HALF), F32), V((80, 128), F32), V((8, 80, 128), BF16), V((8, 80, 128), BF16),
+        V((2, 48, 128), BF16), V((2, 48, 128), BF16),
         dma((9,)),
         dma((3, N)), dma((3, N)),
         dma((8,)), dma((N,)), dma((8,)), dma((8,)), dma((8,)), dma((8,)), dma((8,)),
-        dma((3,)), dma((3,)), dma((7,)), dma((7,)),
+        dma((3,)), dma((3,)), dma((8,)), dma((8,)),
         dma((2, 8)), dma((2, 8)), dma((8,)), dma((8,)), dma((N,)), dma((N,)), dma((N,)), dma((N,)),
+        dma((8,)), dma((8,)), dma((2,)), dma((2,)),
     ]
     shapes = (
         jax.ShapeDtypeStruct((CELLS, W), BF16),
@@ -710,14 +765,14 @@
     made = pl.pallas_call(
         kernel,
         out_shape=shapes,
-        in_specs=[hbm, vmem, hbm, hbm, hbm, hbm, hbm, hbm],
+        in_specs=[hbm, pl.BlockSpec(memory_space=pltpu.SMEM), hbm, hbm, hbm, hbm, hbm, hbm],
         out_specs=(hbm, hbm, vmem, vmem),
         scratch_shapes=scratch,
         compiler_params=pltpu.CompilerParams(
             collective_id=0, has_side_effects=True, vmem_limit_bytes=60 * 1024 * 1024
         ),
     )(
-        features.reshape(CELLS, W), tfeat, upstream.reshape(CELLS, W),
+        features.reshape(CELLS, W), timestep, upstream.reshape(CELLS, W),
         w_time, w_emb, w_qkv, w_out, w_conv,
     )
     out, gf, gc, go = pl.pallas_call(

time: 93.3 us -> 90.4 us (0.969)
  Pallas kernels: 91.1 us -> 89 us
    pallas_call x1, Pallas kernels: 89.3 us -> 87.2 us  [on_device(): pl.pallas_call(kernel, out_shape=shapes, in_specs=[hbm, pl.BlockSpec(memo...]
where the time goes in v4:
time: 90.4 us; the launch traced here: 90.3 us
  Pallas kernels  89 us (98%)
  between operations  1.29 us (1%)
    pallas_call x1, Pallas kernels, on_device(): pl.pallas_call(kernel, out_shape=shapes, in_specs=[hbm, pl.BlockSpec(memo...  87.2 us
    pallas_call x1, Pallas kernels, on_device(): pl.pallas_call(hand_on, out_shape=shapes, in_specs=[hbm] * 4, out_specs=(...  1.81 us

profile of v4, /device:TPU:1, one launch (start us, length us, event | category | flops | bytes accessed | tf_op | source)
XLA Modules:
  0.0 90.3 jit_solution(3456222914283591502)
XLA Ops:
  1.3 87.2 %shard_map.111 = (bf16[256,512]{1,0:T(8,128)(2,1)}, bf16[256,512]{1,0:T(8,128)(2,1)}, f32[72,128]{1,0:T(8,128)}, f32[8,128]{1,0:T(8,128)}) custom-call(bf16[256,512]{1,0:T(8,128)(2,1)} %bitcast.6, s32[1]{0:T(128)S(6)} %copy.12.t_ref, bf16[256,512]{1,0:T(8,128)(2,1)} %bitcast.7, bf16[128,512]{1,0:T(8,128)(2,1)} %wtime_hbm.1, bf16[512,1024]{1,0:T(8,128)(2,1)} %wemb_hbm.1, ...), custom_call_target="tpu_custom_call" | custom-call | tf_op jit(solution)/shard_map/pallas_call | solution.py:765
  88.5 1.8 %shard_map.112 = (bf16[256,512]{1,0:T(8,128)(2,1)}, bf16[256,512]{1,0:T(8,128)(2,1)}, f32[72,128]{1,0:T(8,128)}, f32[8,128]{1,0:T(8,128)}) custom-call(bf16[256,512]{1,0:T(8,128)(2,1)} %get-tuple-element.12.refs_0_, bf16[256,512]{1,0:T(8,128)(2,1)} %get-tuple-element.13.refs_1_, f32[72,128]{1,0:T(8,128)} %get-tuple-element.14.refs_2_, ...), custom_call_target="tpu_custom_call" | custom-call | tf_op jit(solution)/shard_map/pallas_call | solution.py:778

commit v5 on v4

--- a/solution.py
+++ b/solution.py
@@ -133,7 +133,7 @@
     hid, hx, hfar, actp, xact, amat, patt, gf_ref, pgf, actt, attt,
     out_ref, hat, zed, back, thr, mod,
     gst, grecv, gost, gorecv, sum2, piece32, piece, precv, opiece, oprecv,
-    wide32, pack32, zpiece, zrecv, fpiece, frecv,
+    wide32, pack32, zpiece, zrecv, fpiece, frecv, owned,
     lsem,
     st_ssem, st_rsem,
     kv_ssem, kv_rsem, fw_ssem, q_ssem, q_rsem, at_ssem, at_rsem,
@@ -546,12 +546,12 @@
 
     near_chips(lambda to: grad_copy(1, to).start())
     rows_afar = gst[pl.ds(pl.multiple_of(576 * afar + 288 * core, 32), 288), :]
-    wide32[...] = rows_afar.astype(F32)
+    wide32[0:288, :] = rows_afar.astype(F32)
     pack32[...] = jnp.zeros_like(pack32)
     for i in range(8):
         for q in range(2):
             pack32[pl.ds(q, 36, stride=2), :] = wide32[36 * i : 36 * i + 36, 128 * q : 128 * q + 128]
-        zpiece[i] = pack32[...].astype(BF16)
+        zpiece[i] = pack32[0:80, :].astype(BF16)
 
     def z_copy(k):
         h = lax.rem(z + k, 8)
@@ -584,7 +584,7 @@
         grecv[chip, 144 * half : 144 * half + 144] = gst[
             pl.ds(pl.multiple_of(576 * chip + 288 * core + 144 * half, 16), 144), :
         ]
-        sum2[...] = jnp.sum(grecv[:, 144 * half : 144 * half + 144].astype(F32), axis=0)
+        sum2[0:144, :] = jnp.sum(grecv[:, 144 * half : 144 * half + 144].astype(F32), axis=0)
         for i in range(8):
             t = 8 * half + i
             for q in range(2):
@@ -615,7 +615,7 @@
         rcopy(zpiece.at[h], zrecv.at[h], z_ssem.at[h], z_rsem.at[h], other).wait_recv()
 
     loop(1, 8, take_z)
-    pack32[...] = jnp.sum(zrecv[...].astype(F32), axis=0)
+    pack32[0:80, :] = jnp.sum(zrecv[...].astype(F32), axis=0)
 
     def far_copy(side):
         return rcopy(
@@ -700,7 +700,9 @@
             total += precv[2 * i + side].astype(F32)
         piece32[...] = total
         for q in range(2):
-            gc_ref[pl.ds(2 * side + q, 18, stride=4), :] = piece32[pl.ds(q, 18, stride=2), :]
+            owned[pl.ds(2 * side + q, 18, stride=4), :] = piece32[pl.ds(q, 18, stride=2), :]
+
+    gc_ref[...] = owned[0:72, :]
 
     def take_opieces(k):
         t = lax.rem(s + k, N)
@@ -745,10 +747,10 @@
         V((CELLS, W), BF16), V((CELLS, W), F32), V((CELLS, W), F32), V((CELLS, W), F32), V((CELLS, W), F32),
         V((8, 2 * W), F32),
         V((9 * W, HALF), BF16), V((8, 288, HALF), BF16), V((W, W), BF16), V((8, 32, W), BF16),
-        V((144, HALF), F32), V((48, 128), F32), V((N, 48, 128), BF16), V((N, 48, 128), BF16),
+        V((152, HALF), F32), V((48, 128), F32), V((N, 48, 128), BF16), V((N, 48, 128), BF16),
         V((N, 8, 128), F32), V((N, 8, 128), F32),
-        V((288, HALF), F32), V((80, 128), F32), V((8, 80, 128), BF16), V((8, 80, 128), BF16),
-        V((2, 48, 128), BF16), V((2, 48, 128), BF16),
+        V((296, HALF), F32), V((88, 128), F32), V((8, 80, 128), BF16), V((8, 80, 128), BF16),
+        V((2, 48, 128), BF16), V((2, 48, 128), BF16), V((104, 128), F32),
         dma((9,)),
         dma((3, N)), dma((3, N)),
         dma((8,)), dma((N,)), dma((8,)), dma((8,)), dma((8,)), dma((8,)), dma((8,)),

time: 90.4 us -> 90.4 us (level)
  no operation moved by 1% of the time
where the time goes in v5:
time: 90.4 us; the launch traced here: 90.3 us
  Pallas kernels  89 us (98%)
  between operations  1.29 us (1%)
    pallas_call x1, Pallas kernels, on_device(): pl.pallas_call(kernel, out_shape=shapes, in_specs=[hbm, pl.BlockSpec(memo...  87.2 us
    pallas_call x1, Pallas kernels, on_device(): pl.pallas_call(hand_on, out_shape=shapes, in_specs=[hbm] * 4, out_specs=(...  1.81 us

profile of v5, /device:TPU:1, one launch (start us, length us, event | category | flops | bytes accessed | tf_op | source)
XLA Modules:
  0.0 90.3 jit_solution(3922594841435807238)
XLA Ops:
  1.3 87.2 %shard_map.111 = (bf16[256,512]{1,0:T(8,128)(2,1)}, bf16[256,512]{1,0:T(8,128)(2,1)}, f32[72,128]{1,0:T(8,128)}, f32[8,128]{1,0:T(8,128)}) custom-call(bf16[256,512]{1,0:T(8,128)(2,1)} %bitcast.6, s32[1]{0:T(128)S(6)} %copy.12.t_ref, bf16[256,512]{1,0:T(8,128)(2,1)} %bitcast.7, bf16[128,512]{1,0:T(8,128)(2,1)} %wtime_hbm.1, bf16[512,1024]{1,0:T(8,128)(2,1)} %wemb_hbm.1, ...), custom_call_target="tpu_custom_call" | custom-call | tf_op jit(solution)/shard_map/pallas_call | solution.py:767
  88.4 1.8 %shard_map.112 = (bf16[256,512]{1,0:T(8,128)(2,1)}, bf16[256,512]{1,0:T(8,128)(2,1)}, f32[72,128]{1,0:T(8,128)}, f32[8,128]{1,0:T(8,128)}) custom-call(bf16[256,512]{1,0:T(8,128)(2,1)} %get-tuple-element.12.refs_0_, bf16[256,512]{1,0:T(8,128)(2,1)} %get-tuple-element.13.refs_1_, f32[72,128]{1,0:T(8,128)} %get-tuple-element.14.refs_2_, ...), custom_call_target="tpu_custom_call" | custom-call | tf_op jit(solution)/shard_map/pallas_call | solution.py:780
